TPU v7x, 128 devices: a whole 4x4x4 slice. The times are simulated.
128 devices in a mesh: seq: 32 (over y, z, core), head: 4 (over x).
Axes of the slice: x: 4, y: 4, z: 4, core: 2. Of those that a mesh axis runs over, the one named last changes fastest.
Arguments:
- queries: bfloat16 [4096, 128, 576], P('seq', 'head'), may hold values from -400 to 400
- cache: bfloat16 [65536, 576], P('seq'), may hold values from -9 to 9
- d_out: bfloat16 [4096, 128, 512], P('seq', 'head'), may hold values from -6 to 6
- picks: int32 [4096, 6], P('seq'), may hold values from 0 to 1023, as said below
- q_pos: int32 [4096], P('seq'), may hold values from 32768 to 65535, as said below
Outputs:
- attended_out: bfloat16 [4096, 128, 512], P('seq', 'head')
- d_queries: bfloat16 [4096, 128, 576], P('seq', 'head')
- d_cache: float32 [65536, 576], P(('seq', 'head'))
Inputs may be any that keep to these rules, and one draw needn't show every extreme that they name: `picks`: row q names 6 different blocks: the first holds position q_pos[q], the others lie wholly before it. The rows of one aligned run of 128 queries name at most 4 distinct blocks within one aligned range of 2048 cache tokens, and exactly 4 in some range of every draw. `q_pos`: each aligned run of 128 queries holds consecutive positions beginning at a multiple of 128.
All inputs are finite; a program needn't handle non-finite values.
Results may differ from a plain program's by a relative error of at most 0.015.
Values may be sent and summed in bfloat16 or wider, within the bound.
A program may use at most 256 MiB of HBM per device.

v0:
```python
import math

import jax
import jax.numpy as jnp
from jax import lax
from jax.sharding import PartitionSpec as P

BLOCK = 64
POOL = 64


score_scale = 1.0 / math.sqrt(192.0)
masked_score = -1e30


def attend_rows(query_rows, gathered_keys, key_pos, pos_rows, grad_rows):
    lat_width = grad_rows.shape[2]
    scores = (
        jnp.einsum("bhc,bkc->bhk", query_rows, gathered_keys, preferred_element_type=jnp.float32)
        * score_scale
    )
    visible = key_pos[:, None, :] <= pos_rows[:, None, None]
    scores = jnp.where(visible, scores, masked_score)
    row_max = jnp.max(scores, axis=2, keepdims=True)
    exp_scores = jnp.exp(scores - row_max)
    softmax_probs = exp_scores / jnp.sum(exp_scores, axis=2, keepdims=True)
    weights = softmax_probs.astype(jnp.bfloat16)
    latent_values = gathered_keys[:, :, :lat_width]
    attended = jnp.einsum(
        "bhk,bkl->bhl", weights, latent_values, preferred_element_type=jnp.float32
    )
    row_delta = jnp.sum(grad_rows.astype(jnp.float32) * attended, axis=2, keepdims=True)
    d_prob = jnp.einsum(
        "bhl,bkl->bhk", grad_rows, latent_values, preferred_element_type=jnp.float32
    )
    d_score = (softmax_probs * (d_prob - row_delta)).astype(jnp.bfloat16)
    d_query = (
        jnp.einsum("bhk,bkc->bhc", d_score, gathered_keys, preferred_element_type=jnp.float32)
        * score_scale
    )
    d_key = (
        jnp.einsum("bhk,bhc->bkc", d_score, query_rows, preferred_element_type=jnp.float32)
        * score_scale
    )
    d_value = jnp.einsum("bhk,bhl->bkl", weights, grad_rows, preferred_element_type=jnp.float32)
    rope_zeros = jnp.zeros(d_key.shape[:2] + (d_key.shape[2] - lat_width,), jnp.float32)
    d_key = d_key + jnp.concatenate([d_value, rope_zeros], axis=2)
    return (attended.astype(jnp.bfloat16), d_query.astype(jnp.bfloat16), d_key)


def on_device(queries, cache, d_out, picks, q_pos):
    seq_count = lax.axis_size("seq")
    rows_dev, heads_dev, key_width = queries.shape
    ctx_rows = cache.shape[0]
    blocks_dev = ctx_rows // BLOCK
    per_owner = POOL // seq_count + rows_dev // BLOCK
    all_blocks = seq_count * blocks_dev
    slot_total = seq_count * per_owner
    flat_picks = picks.reshape(-1)
    block_ids = jnp.arange(all_blocks, dtype=jnp.int32)
    matches = flat_picks[:, None] == block_ids[None, :]
    present = jnp.any(matches, axis=0).reshape(seq_count, blocks_dev)
    block_ranks = jnp.cumsum(present.astype(jnp.int32), axis=1) - 1
    slot_table = (
        jnp.arange(seq_count, dtype=jnp.int32)[:, None] * per_owner + block_ranks
    ).reshape(-1)
    slot_picks = jnp.sum(jnp.where(matches, slot_table[None, :], 0), axis=1).reshape(picks.shape)
    slot_hits = present[:, None, :] & (
        block_ranks[:, None, :] == jnp.arange(per_owner, dtype=jnp.int32)[None, :, None]
    )
    wanted = jnp.sum(
        jnp.where(slot_hits, jnp.arange(blocks_dev, dtype=jnp.int32)[None, None, :], 0), axis=2
    )
    asked_blocks = lax.all_to_all(wanted, "seq", split_axis=0, concat_axis=0, tiled=True)
    targets = asked_blocks.reshape(-1)
    target_onehot = targets[:, None] == jnp.arange(blocks_dev, dtype=jnp.int32)[None, :]
    cache_flat = cache.reshape(blocks_dev, BLOCK * key_width)
    served = jnp.dot(
        target_onehot.astype(jnp.bfloat16), cache_flat, preferred_element_type=jnp.float32
    ).astype(jnp.bfloat16)
    served = served.reshape(seq_count, per_owner, BLOCK, key_width)
    fetched = lax.all_to_all(served, "seq", split_axis=0, concat_axis=0, tiled=True)
    fetched_flat = fetched.reshape(slot_total, BLOCK * key_width)
    batch_rows = 16
    offsets = jnp.arange(BLOCK, dtype=jnp.int32)
    slot_ids = jnp.arange(slot_total, dtype=jnp.int32)

    def attend_batch(slot_grads, first_row):
        query_rows = lax.dynamic_slice_in_dim(queries, first_row, batch_rows, 0)
        grad_rows = lax.dynamic_slice_in_dim(d_out, first_row, batch_rows, 0)
        pos_rows = lax.dynamic_slice_in_dim(q_pos, first_row, batch_rows, 0)
        pick_rows = lax.dynamic_slice_in_dim(picks, first_row, batch_rows, 0)
        slot_rows = lax.dynamic_slice_in_dim(slot_picks, first_row, batch_rows, 0)
        slot_onehot = (slot_rows[:, :, None] == slot_ids[None, None, :]).reshape(-1, slot_total)
        key_pos = (pick_rows[:, :, None] * BLOCK + offsets[None, None, :]).reshape(batch_rows, -1)
        gathered_keys = jnp.dot(
            slot_onehot.astype(jnp.bfloat16), fetched_flat, preferred_element_type=jnp.float32
        ).astype(jnp.bfloat16)
        gathered_keys = gathered_keys.reshape(batch_rows, -1, key_width)
        attended, d_query, d_key = attend_rows(
            query_rows, gathered_keys, key_pos, pos_rows, grad_rows
        )
        key_terms = d_key.reshape(-1, BLOCK * key_width)
        slot_grads = slot_grads + jnp.dot(
            slot_onehot.astype(jnp.float32).T,
            key_terms,
            precision=lax.Precision.HIGHEST,
            preferred_element_type=jnp.float32,
        )
        return (slot_grads, (attended, d_query))

    starts = jnp.arange(rows_dev // batch_rows, dtype=jnp.int32) * batch_rows
    slot_grads, (outputs, d_queries) = lax.scan(
        attend_batch, jnp.zeros((slot_total, BLOCK * key_width), jnp.float32), starts
    )
    outputs = outputs.reshape(rows_dev, heads_dev, -1)
    d_queries = d_queries.reshape(rows_dev, heads_dev, key_width)
    slot_grads = slot_grads.reshape(seq_count, per_owner, BLOCK, key_width)
    owner_map = target_onehot.astype(jnp.float32).T
    returned = lax.all_to_all(
        slot_grads.astype(jnp.bfloat16), "seq", split_axis=0, concat_axis=0, tiled=True
    ).astype(slot_grads.dtype)
    owned_grads = jnp.dot(
        owner_map,
        returned.reshape(slot_total, BLOCK * key_width),
        precision=lax.Precision.HIGHEST,
        preferred_element_type=jnp.float32,
    )
    d_cache = lax.psum_scatter(
        owned_grads.reshape(ctx_rows, key_width).astype(jnp.bfloat16),
        "head",
        scatter_dimension=0,
        tiled=True,
    ).astype(jnp.float32)
    return (outputs, d_queries, d_cache)


def solution(mesh):
    placed = (
        P("seq", "head", None),
        P("seq", None),
        P("seq", "head", None),
        P("seq", None),
        P("seq"),
    )
    return jax.shard_map(
        on_device,
        mesh=mesh,
        in_specs=placed,
        out_specs=(P("seq", "head", None), P("seq", "head", None), P(("seq", "head"), None)),
        check_vma=False,
    )
```

profile of v0, /device:TPU:1, one launch (start us, length us, event | category | flops | bytes accessed | tf_op | source)
XLA Modules:
  0.0 1447.1 jit_solution(8470829873095522697)
XLA Ops:
  34.6 18.4 %reshape.120 = bf16[32,4,64,576]{3,2,1,0:T(8,128)(2,1)} reshape(bf16[128,36864]{1,0:T(8,128)(2,1)} %convolution_convert_fusion.1) | data formatting | bytes 18874368 | tf_op jit(solution)/shard_map/reshape | solution.py:81
  70.3 133.7 %all-to-all-done.1 = bf16[32,4,64,576]{3,2,1,0:T(8,128)(2,1)} async-done(((bf16[32,4,64,576]{3,2,1,0:T(8,128)(2,1)}), bf16[32,4,64,576]{3,2,1,0:T(8,128)(2,1)}, u32[]{:S(2)}, u32[]{:S(2)}) %all-to-all-start.1) | async-done | bytes 9437216 | tf_op jit(solution)/shard_map/all_to_all | solution.py:82
  203.9 18.5 %reshape.121 = bf16[128,36864]{1,0:T(8,128)(2,1)} reshape(bf16[32,4,64,576]{3,2,1,0:T(8,128)(2,1)} %all-to-all-done.1) | data formatting | bytes 18874368 | tf_op jit(solution)/shard_map/reshape | solution.py:83
  222.4 981.3 %while.15 = (s32[]{:T(128)}, f32[128,36864]{1,0:T(8,128)}, bf16[8,16,32,512]{3,2,1,0:T(8,128)(2,1)}, bf16[8,16,32,576]{3,2,1,0:T(8,128)(2,1)}, s32[8]{0:T(128)S(...) while((s32[]{:T(128)}, f32[128,36864]{1,0:T(8,128)}, ...), condition=%wide.region_8.9_spmd.clone, body=%wide.region_4.8_spmd.clone.sunk | while | flops 7649728512 | bytes 219559728 | solution.py:113
  291.8 14.2 copy.53
  306.0 17.5 %reshape.139 = f32[96,36864]{1,0:T(8,128)} reshape(f32[16,384,576]{2,1,0:T(8,128)} %copy.53) | data formatting | bytes 28311552 | tf_op jit(solution)/shard_map/while/body/eval_jaxpr/reshape | solution.py:103
  323.5 17.1 %convolution_add_fusion.2 = f32[128,36864]{1,0:T(8,128)} fusion(f32[96,36864]{1,0:T(8,128)} %reshape.139, f32[128,36864]{1,0:T(8,128)} %get-tuple-element.294, pred[]{:T(512)S(6)} %compare.4, s32[96]{0:T(128)S(1)} %eq.131), kind=kOutput, calls=%fused_computation.3.clone.1 | convolution fusion | flops 5445267456 | bytes 51904896 | tf_op jit(solution)/shard_map/while/body/eval_jaxpr/dot_general | solution.py:104
  409.9 14.2 copy.53
  424.2 17.5 %reshape.139 = f32[96,36864]{1,0:T(8,128)} reshape(f32[16,384,576]{2,1,0:T(8,128)} %copy.53) | data formatting | bytes 28311552 | tf_op jit(solution)/shard_map/while/body/eval_jaxpr/reshape | solution.py:103
  441.6 22.2 %convolution_add_fusion.2 = f32[128,36864]{1,0:T(8,128)} fusion(f32[96,36864]{1,0:T(8,128)} %reshape.139, f32[128,36864]{1,0:T(8,128)} %get-tuple-element.294, pred[]{:T(512)S(6)} %compare.4, s32[96]{0:T(128)S(1)} %eq.131), kind=kOutput, calls=%fused_computation.3.clone.1 | convolution fusion | flops 5445267456 | bytes 51904896 | tf_op jit(solution)/shard_map/while/body/eval_jaxpr/dot_general | solution.py:104
  533.2 14.2 copy.53
  547.5 17.5 %reshape.139 = f32[96,36864]{1,0:T(8,128)} reshape(f32[16,384,576]{2,1,0:T(8,128)} %copy.53) | data formatting | bytes 28311552 | tf_op jit(solution)/shard_map/while/body/eval_jaxpr/reshape | solution.py:103
  564.9 22.2 %convolution_add_fusion.2 = f32[128,36864]{1,0:T(8,128)} fusion(f32[96,36864]{1,0:T(8,128)} %reshape.139, f32[128,36864]{1,0:T(8,128)} %get-tuple-element.294, pred[]{:T(512)S(6)} %compare.4, s32[96]{0:T(128)S(1)} %eq.131), kind=kOutput, calls=%fused_computation.3.clone.1 | convolution fusion | flops 5445267456 | bytes 51904896 | tf_op jit(solution)/shard_map/while/body/eval_jaxpr/dot_general | solution.py:104
  656.5 14.2 copy.53
  670.7 17.5 %reshape.139 = f32[96,36864]{1,0:T(8,128)} reshape(f32[16,384,576]{2,1,0:T(8,128)} %copy.53) | data formatting | bytes 28311552 | tf_op jit(solution)/shard_map/while/body/eval_jaxpr/reshape | solution.py:103
  688.2 22.2 %convolution_add_fusion.2 = f32[128,36864]{1,0:T(8,128)} fusion(f32[96,36864]{1,0:T(8,128)} %reshape.139, f32[128,36864]{1,0:T(8,128)} %get-tuple-element.294, pred[]{:T(512)S(6)} %compare.4, s32[96]{0:T(128)S(1)} %eq.131), kind=kOutput, calls=%fused_computation.3.clone.1 | convolution fusion | flops 5445267456 | bytes 51904896 | tf_op jit(solution)/shard_map/while/body/eval_jaxpr/dot_general | solution.py:104
  779.8 14.2 copy.53
  794.0 17.5 %reshape.139 = f32[96,36864]{1,0:T(8,128)} reshape(f32[16,384,576]{2,1,0:T(8,128)} %copy.53) | data formatting | bytes 28311552 | tf_op jit(solution)/shard_map/while/body/eval_jaxpr/reshape | solution.py:103
  811.5 22.2 %convolution_add_fusion.2 = f32[128,36864]{1,0:T(8,128)} fusion(f32[96,36864]{1,0:T(8,128)} %reshape.139, f32[128,36864]{1,0:T(8,128)} %get-tuple-element.294, pred[]{:T(512)S(6)} %compare.4, s32[96]{0:T(128)S(1)} %eq.131), kind=kOutput, calls=%fused_computation.3.clone.1 | convolution fusion | flops 5445267456 | bytes 51904896 | tf_op jit(solution)/shard_map/while/body/eval_jaxpr/dot_general | solution.py:104
  903.1 14.2 copy.53
  917.3 17.5 %reshape.139 = f32[96,36864]{1,0:T(8,128)} reshape(f32[16,384,576]{2,1,0:T(8,128)} %copy.53) | data formatting | bytes 28311552 | tf_op jit(solution)/shard_map/while/body/eval_jaxpr/reshape | solution.py:103
  934.8 22.2 %convolution_add_fusion.2 = f32[128,36864]{1,0:T(8,128)} fusion(f32[96,36864]{1,0:T(8,128)} %reshape.139, f32[128,36864]{1,0:T(8,128)} %get-tuple-element.294, pred[]{:T(512)S(6)} %compare.4, s32[96]{0:T(128)S(1)} %eq.131), kind=kOutput, calls=%fused_computation.3.clone.1 | convolution fusion | flops 5445267456 | bytes 51904896 | tf_op jit(solution)/shard_map/while/body/eval_jaxpr/dot_general | solution.py:104
  1026.4 14.2 copy.53
  1040.7 17.5 %reshape.139 = f32[96,36864]{1,0:T(8,128)} reshape(f32[16,384,576]{2,1,0:T(8,128)} %copy.53) | data formatting | bytes 28311552 | tf_op jit(solution)/shard_map/while/body/eval_jaxpr/reshape | solution.py:103
  1058.1 22.2 %convolution_add_fusion.2 = f32[128,36864]{1,0:T(8,128)} fusion(f32[96,36864]{1,0:T(8,128)} %reshape.139, f32[128,36864]{1,0:T(8,128)} %get-tuple-element.294, pred[]{:T(512)S(6)} %compare.4, s32[96]{0:T(128)S(1)} %eq.131), kind=kOutput, calls=%fused_computation.3.clone.1 | convolution fusion | flops 5445267456 | bytes 51904896 | tf_op jit(solution)/shard_map/while/body/eval_jaxpr/dot_general | solution.py:104
  1149.7 14.2 copy.53
  1164.0 17.5 %reshape.139 = f32[96,36864]{1,0:T(8,128)} reshape(f32[16,384,576]{2,1,0:T(8,128)} %copy.53) | data formatting | bytes 28311552 | tf_op jit(solution)/shard_map/while/body/eval_jaxpr/reshape | solution.py:103
  1181.4 22.2 %convolution_add_fusion.2 = f32[128,36864]{1,0:T(8,128)} fusion(f32[96,36864]{1,0:T(8,128)} %reshape.139, f32[128,36864]{1,0:T(8,128)} %get-tuple-element.294, pred[]{:T(512)S(6)} %compare.4, s32[96]{0:T(128)S(1)} %eq.131), kind=kOutput, calls=%fused_computation.3.clone.1 | convolution fusion | flops 5445267456 | bytes 51904896 | tf_op jit(solution)/shard_map/while/body/eval_jaxpr/dot_general | solution.py:104
  1214.9 18.4 %convert_element_type.47 = bf16[32,4,64,576]{3,2,1,0:T(8,128)(2,1)} reshape(bf16[128,36864]{1,0:T(8,128)(2,1)} %convert_element_type.46) | data formatting | bytes 18874368 | tf_op jit(solution)/shard_map/convert_element_type | solution.py:121
  1233.3 145.0 %all_to_all.19 = bf16[32,4,64,576]{3,2,1,0:T(8,128)(2,1)} all-to-all(bf16[32,4,64,576]{3,2,1,0:T(8,128)(2,1)} %convert_element_type.47), channel_id=1, replica_groups=mesh['seq'=32,'head'=4] {'seq'}, dimensions={0} | all-to-all | bytes 18874368 | tf_op jit(solution)/shard_map/all_to_all | solution.py:120
  1378.3 18.6 %reshape.124 = bf16[128,36864]{1,0:T(8,128)(2,1)} reshape(bf16[32,4,64,576]{3,2,1,0:T(8,128)(2,1)} %all_to_all.19) | data formatting | bytes 18874368 | tf_op jit(solution)/shard_map/reshape | solution.py:125
  1414.9 23.0 %reduce-scatter.2.cloned.1.call-done = bf16[512,576]{1,0:T(8,128)(2,1)} async-done(((bf16[2048,576]{1,0:T(8,128)(2,1)}), bf16[512,576]{1,0:T(8,128)(2,1)}) %reduce-scatter.2.cloned.1.call-update) | async-done | bytes 589840 | tf_op jit(solution)/shard_map/reduce_scatter | solution.py:129
  (192 shorter events, 616.0 us)
Async XLA Ops:
  9.8 16.7 %all-to-all-start = ((s32[32,1,4]{2,1,0:T(1,128)}), s32[32,1,4]{2,1,0:T(1,128)S(1)}, u32[]{:S(2)}, u32[]{:S(2)}) async-start(s32[32,1,4]{2,1,0:T(1,128)} %copy.43), calls=%async_computation | async-start | bytes 32768 | tf_op jit(solution)/shard_map/all_to_all | solution.py:74
  27.9 25.2 %copy-start = (s32[128]{0:T(128)}, s32[128]{0:T(128)S(1)}, u32[]{:S(2)}) copy-start(s32[128]{0:T(128)S(1)} %eq.66) | copy-start | bytes 1540
  53.0 150.9 %all-to-all-start.1 = ((bf16[32,4,64,576]{3,2,1,0:T(8,128)(2,1)}), bf16[32,4,64,576]{3,2,1,0:T(8,128)(2,1)}, u32[]{:S(2)}, u32[]{:S(2)}) async-start(bf16[32,4,64,576]{3,2,1,0:T(8,128)(2,1)} %reshape.120), calls=%async_computation.1 | async-start | bytes 20971520 | tf_op jit(solution)/shard_map/all_to_all | solution.py:82
  60.4 1377.4 %reduce-scatter.2.cloned.1.call-start = ((), (), s32[]{:S(2)}) async-start(), calls=%async_computation.4 | async-start | bytes 3276800 | tf_op jit(solution)/shard_map/reduce_scatter | solution.py:129
  70.3 152.1 %copy-start.2 = (s32[128]{0:T(128)S(1)}, s32[128]{0:T(128)}, u32[]{:S(2)}) copy-start(s32[128]{0:T(128)} %param.11) | copy-start | bytes 1540
  1378.3 18.6 %copy-start.1 = (s32[128]{0:T(128)S(1)}, s32[128]{0:T(128)}, u32[]{:S(2)}) copy-start(s32[128]{0:T(128)} %copy-done) | copy-start | bytes 1540
Sparse Core Ops, SparseCore 0:
  1406.3 31.5 reduce-scatter.1
where the time goes:
time: 1460 us; the launch traced here: 1450 us
  matrix products  574 us (39%)
  local copies, waits for them, and re-layouts  489 us (33%)
  waiting for transfers between devices  157 us (11%)
  blocking collectives  145 us (10%)
  other arithmetic  36.4 us (2%)
  starting transfers between devices  17.1 us (1%)
  loops' own time  15 us (1%)
    dot_general x8, matrix products, attend_batch(): jnp.dot(slot_onehot.astype(jnp.float32).T, key_terms, precision=lax.Preci...  173 us
    all_to_all x1, blocking collectives, on_device(): lax.all_to_all(slot_grads.astype(jnp.bfloat16), 'seq', split_axis=0, conc...  145 us
    reshape x8, local copies, waits for them, and re-layouts, attend_batch(): key_terms = d_key.reshape(-1, BLOCK * key_width)  140 us
    all_to_all x1, waiting for transfers between devices, on_device(): lax.all_to_all(served, 'seq', split_axis=0, concat_axis=0, tiled=True)  134 us
    add x8, local copies, waits for them, and re-layouts, attend_rows(): d_key = d_key + jnp.concatenate([d_value, rope_zeros], axis=2)  114 us
    reshape x8, local copies, waits for them, and re-layouts, attend_batch(): gathered_keys = gathered_keys.reshape(batch_rows, -1, key_width)  113 us
    dot_general x8, matrix products, attend_rows(): jnp.einsum('bhk,bhc->bkc', d_score, query_rows, preferred_element_type=jn...  95.1 us
    dot_general x8, matrix products, attend_batch(): jnp.dot(slot_onehot.astype(jnp.bfloat16), fetched_flat, preferred_element...  68.5 us
  transfers between devices with their start and end apart: 3, of which 2 were waited for; matrix products, arithmetic and copies ran while one was open for 2% of the time, Pallas kernels for 0%

commit v1 on v0

v1 whole, which is shorter than its diff:
```python
import functools
import math

import jax
import jax.numpy as jnp
from jax import lax
from jax.experimental import pallas as pl
from jax.experimental.pallas import tpu as pltpu
from jax.sharding import PartitionSpec as P

BLOCK = 64
POOL = 64
NSEL = 6

score_scale = 1.0 / math.sqrt(192.0)
masked_score = -1e30

BF16 = jnp.bfloat16
F32 = jnp.float32
COPY_ROWS = 16
STEP_ROWS = 8
CHUNK = 8
HBM = pl.BlockSpec(memory_space=pl.ANY)
SMEM = pl.BlockSpec(memory_space=pltpu.SMEM)
VMEM = pl.BlockSpec(memory_space=pltpu.VMEM)
VMEM_BYTES = 60 * 2**20


def take_blocks_kernel(index_ref, src, dst, sems):
    def copy(i):
        return pltpu.make_async_copy(src.at[index_ref[i]], dst.at[i], sems.at[i])

    def start(i, c):
        copy(i).start()
        return c

    def wait(i, c):
        copy(i).wait()
        return c

    lax.fori_loop(0, dst.shape[0], start, 0)
    lax.fori_loop(0, dst.shape[0], wait, 0)


def take_blocks(index, blocks):
    count = index.shape[0]
    return pl.pallas_call(
        take_blocks_kernel,
        out_shape=jax.ShapeDtypeStruct((count,) + blocks.shape[1:], blocks.dtype),
        in_specs=[SMEM, VMEM],
        out_specs=HBM,
        scratch_shapes=[pltpu.SemaphoreType.DMA((count,))],
        compiler_params=pltpu.CompilerParams(vmem_limit_bytes=VMEM_BYTES),
        name="take_blocks",
    )(index, blocks)


def add_blocks_kernel(asked_ref, src, out, total):
    total[...] = jnp.zeros_like(total)

    def add(i, c):
        block = asked_ref[i]

        @pl.when(block >= 0)
        def _():
            total[block] += src[i].astype(F32)

        return c

    lax.fori_loop(0, src.shape[0], add, 0)
    out[...] = total[...].astype(out.dtype)


def add_blocks(asked, returned, blocks_dev):
    shape = (blocks_dev,) + returned.shape[1:]
    return pl.pallas_call(
        add_blocks_kernel,
        out_shape=jax.ShapeDtypeStruct(shape, BF16),
        in_specs=[SMEM, VMEM],
        out_specs=VMEM,
        scratch_shapes=[pltpu.VMEM(shape, F32)],
        compiler_params=pltpu.CompilerParams(vmem_limit_bytes=VMEM_BYTES),
        name="add_blocks",
    )(asked, returned)


def attend_kernel(
    count_ref, slot_ref, limit_ref, q_hbm, g_hbm, k1_hbm, k2_hbm,
    o_hbm, dq_hbm, dk1_hbm, dk2_hbm,
    q_v, g_v, k_v, o_v, dq_v, dk_v, y_v, kt_v, acc_v, cnt, lst,
    sem_in, sem_k, sem_out, sem_dk,
):
    rows, heads, width = q_v.shape
    lat = g_v.shape[2]
    parts, places = k_v.shape[0], k_v.shape[1]
    near = k1_hbm.shape[1]
    groups = rows // COPY_ROWS
    slots = parts * places
    more = count_ref[0] > parts * near

    def in_copies(i):
        s = pl.ds(i * COPY_ROWS, COPY_ROWS)
        return (
            pltpu.make_async_copy(q_hbm.at[s], q_v.at[s], sem_in.at[i, 0]),
            pltpu.make_async_copy(g_hbm.at[s], g_v.at[s], sem_in.at[i, 1]),
        )

    def out_copies(i):
        s = pl.ds(i * COPY_ROWS, COPY_ROWS)
        b = lax.rem(i, 2)
        return (
            pltpu.make_async_copy(o_v.at[b], o_hbm.at[s], sem_out.at[b, 0]),
            pltpu.make_async_copy(dq_v.at[b], dq_hbm.at[s], sem_out.at[b, 1]),
        )

    key_copies = [
        pltpu.make_async_copy(k1_hbm.at[h], k_v.at[h, pl.ds(0, near)], sem_k.at[h])
        for h in range(parts)
    ]
    far_copies = [
        pltpu.make_async_copy(
            k2_hbm.at[h], k_v.at[h, pl.ds(near, places - near)], sem_k.at[parts + h]
        )
        for h in range(parts)
    ]
    for c in key_copies:
        c.start()

    @pl.when(more)
    def _():
        for c in far_copies:
            c.start()

    for i in range(groups):
        for c in in_copies(i):
            c.start()

    def clear(i, c):
        cnt[i] = 0
        return c

    lax.fori_loop(0, slots, clear, 0)
    y_v[rows * NSEL] = jnp.zeros((heads, 2 * BLOCK), BF16)
    for c in key_copies:
        c.wait()

    @pl.when(more)
    def _():
        for c in far_copies:
            c.wait()

    used = jnp.where(more, places, near)

    def turn(place, c):
        for h in range(parts):
            k = k_v[h, place]
            kt_v[place * parts + h] = jnp.concatenate([k, k], 0).T
        return c

    lax.fori_loop(0, used, turn, 0)

    lane = lax.broadcasted_iota(jnp.int32, (1, BLOCK), 1)
    low = lax.broadcasted_iota(jnp.int32, (width, 2 * BLOCK), 1) < BLOCK

    def step(at, group):
        first = group * COPY_ROWS + at * STEP_ROWS
        buf = lax.rem(group, 2)
        products, keys = [], []
        for i in range(STEP_ROWS):
            q = first + i
            picked, turned = [], []
            for j in range(NSEL):
                s = slot_ref[q * NSEL + j]
                c = cnt[s]
                lst[s * rows + c] = q * 8 + j
                cnt[s] = c + 1
                picked.append(k_v[s & 3, s >> 2])
                turned.append(kt_v[s])
            k = jnp.concatenate(picked, 0)
            kt = jnp.concatenate(
                [jnp.where(low, turned[j], turned[j + 1]) for j in range(0, NSEL, 2)], 1
            )
            grad = jnp.concatenate([g_v[q], jnp.zeros((heads, width - lat), BF16)], 1)
            both = jnp.concatenate([q_v[q], grad], 0)
            products.append(jnp.dot(both, kt, preferred_element_type=F32))
            keys.append(k)
        for i in range(STEP_ROWS):
            q = first + i
            scores = products[i][:heads] * score_scale
            d_prob = products[i][heads:]
            own = jnp.where(lane <= limit_ref[q], scores[:, :BLOCK], masked_score)
            scores = jnp.concatenate([own, scores[:, BLOCK:]], 1)
            e = jnp.exp(scores - jnp.max(scores, axis=1, keepdims=True))
            probs = e * (1.0 / jnp.sum(e, axis=1, keepdims=True))
            weights = probs.astype(BF16)
            delta = jnp.sum(weights.astype(F32) * d_prob, axis=1, keepdims=True)
            d_score = (probs * (d_prob - delta) * score_scale).astype(BF16)
            for j in range(NSEL):
                t = slice(j * BLOCK, (j + 1) * BLOCK)
                y_v[q * NSEL + j] = jnp.concatenate([d_score[:, t], weights[:, t]], 1)
            out = jnp.dot(
                jnp.concatenate([d_score, weights], 0), keys[i], preferred_element_type=F32
            )
            dq_v[buf, at * STEP_ROWS + i] = out[:heads].astype(BF16)
            o_v[buf, at * STEP_ROWS + i] = out[heads:, :lat].astype(BF16)
        return group

    def group(i, c):
        for x in in_copies(i):
            x.wait()

        @pl.when(i >= 2)
        def _():
            for x in out_copies(i - 2):
                x.wait()

        lax.fori_loop(0, COPY_ROWS // STEP_ROWS, step, i)
        for x in out_copies(i):
            x.start()
        return c

    lax.fori_loop(0, groups, group, 0)

    def key_step(place):
        names = [place * parts + h for h in range(parts)]
        counts = [cnt[s] for s in names]
        most = functools.reduce(jnp.maximum, counts)

        def chunk(c):
            sums = []
            for s, n in zip(names, counts):
                ys, qs, gs = [], [], []
                for i in range(CHUNK):
                    at = c * CHUNK + i
                    v = lst[s * rows + jnp.minimum(at, rows - 1)]
                    v = jnp.where(at < n, v, rows * 8)
                    q = v >> 3
                    ys.append(y_v[q * NSEL + (v & 7)])
                    q = jnp.minimum(q, rows - 1)
                    qs.append(q_v[q])
                    gs.append(g_v[q])
                y = jnp.concatenate(ys, 0).T
                a = jnp.dot(y[:BLOCK], jnp.concatenate(qs, 0), preferred_element_type=F32)
                b = jnp.dot(y[BLOCK:], jnp.concatenate(gs, 0), preferred_element_type=F32)
                sums.append(jnp.concatenate([a[:, :lat] + b, a[:, lat:]], 1))
            return sums

        for h, r in enumerate(chunk(0)):
            acc_v[h] = r

        def again(c, x):
            for h, r in enumerate(chunk(c)):
                acc_v[h] += r
            return x

        lax.fori_loop(1, (most + CHUNK - 1) // CHUNK, again, 0)

    def key_loop(begin, end, dk_hbm):
        def dk_copy(place):
            b = lax.rem(place, 2)
            return pltpu.make_async_copy(dk_v.at[b], dk_hbm.at[:, place - begin], sem_dk.at[b])

        def body(place, c):
            key_step(place)

            @pl.when(place >= begin + 2)
            def _():
                dk_copy(place - 2).wait()

            dk_v[lax.rem(place, 2)] = acc_v[...].astype(BF16)
            dk_copy(place).start()
            return c

        lax.fori_loop(begin, end, body, 0)
        dk_copy(jnp.int32(end - 2)).wait()
        dk_copy(jnp.int32(end - 1)).wait()

    key_loop(0, near, dk1_hbm)

    @pl.when(more)
    def _():
        key_loop(near, places, dk2_hbm)

    for i in (groups - 2, groups - 1):
        for c in out_copies(jnp.int32(i)):
            c.wait()


def attend(count, slots, limit, queries, d_out, k1, k2):
    rows, heads, width = queries.shape
    lat = d_out.shape[2]
    parts, near = k1.shape[:2]
    places = near + k2.shape[1]
    groups = rows // COPY_ROWS
    return pl.pallas_call(
        attend_kernel,
        out_shape=(
            jax.ShapeDtypeStruct((rows, heads, lat), BF16),
            jax.ShapeDtypeStruct((rows, heads, width), BF16),
            jax.ShapeDtypeStruct(k1.shape, BF16),
            jax.ShapeDtypeStruct(k2.shape, BF16),
        ),
        in_specs=[SMEM, SMEM, SMEM, HBM, HBM, HBM, HBM],
        out_specs=(HBM, HBM, HBM, HBM),
        scratch_shapes=[
            pltpu.VMEM((rows, heads, width), BF16),
            pltpu.VMEM((rows, heads, lat), BF16),
            pltpu.VMEM((parts, places, BLOCK, width), BF16),
            pltpu.VMEM((2, COPY_ROWS, heads, lat), BF16),
            pltpu.VMEM((2, COPY_ROWS, heads, width), BF16),
            pltpu.VMEM((2, parts, BLOCK, width), BF16),
            pltpu.VMEM((rows * NSEL + 1, heads, 2 * BLOCK), BF16),
            pltpu.VMEM((parts * places, width, 2 * BLOCK), BF16),
            pltpu.VMEM((parts, BLOCK, width), F32),
            pltpu.SMEM((parts * places,), jnp.int32),
            pltpu.SMEM((parts * places * rows,), jnp.int32),
            pltpu.SemaphoreType.DMA((groups, 2)),
            pltpu.SemaphoreType.DMA((2 * parts,)),
            pltpu.SemaphoreType.DMA((2, 2)),
            pltpu.SemaphoreType.DMA((2,)),
        ],
        compiler_params=pltpu.CompilerParams(vmem_limit_bytes=VMEM_BYTES),
        name="attend",
    )(count, slots, limit, queries, d_out, k1, k2)


def on_device(queries, cache, d_out, picks, q_pos):
    seq_count = lax.axis_size("seq")
    parts = lax.axis_size("head")
    part = lax.axis_index("head")
    rows, heads, width = queries.shape
    blocks_dev = cache.shape[0] // BLOCK
    all_blocks = seq_count * blocks_dev
    most_blocks = seq_count * 4
    places = most_blocks // parts
    near = -(-(POOL + rows // BLOCK) // parts)

    flat = picks.reshape(-1)
    block_ids = jnp.arange(all_blocks, dtype=jnp.int32)
    matches = flat[:, None] == block_ids[None, :]
    present = jnp.any(matches, axis=0)
    rank = jnp.cumsum(present.astype(jnp.int32)) - 1
    count = rank[-1] + 1
    slots = jnp.sum(jnp.where(matches, rank[None, :], 0), axis=1)
    mine = (present & (rank % parts == part)).reshape(seq_count, blocks_dev)
    wanted = jnp.max(
        jnp.where(mine, jnp.arange(blocks_dev, dtype=jnp.int32)[None, :], -1), axis=1
    )
    place_of = jnp.max(
        jnp.where(mine, rank.reshape(seq_count, blocks_dev) // parts, 0), axis=1
    )
    at_place = present[None, :] & (
        rank[None, :] == (jnp.arange(places, dtype=jnp.int32) * parts + part)[:, None]
    )
    owner_at = jnp.max(jnp.where(at_place, (block_ids // blocks_dev)[None, :], 0), axis=1)

    request = jnp.stack([wanted, jnp.full((seq_count,), count, jnp.int32)], axis=1)
    asked = lax.all_to_all(request, "seq", split_axis=0, concat_axis=0, tiled=True)
    blocks_asked = asked[:, 0]
    overflow = jnp.max(asked[:, 1]) > near * parts

    served = take_blocks(
        jnp.maximum(blocks_asked, 0), cache.reshape(blocks_dev, BLOCK, width)
    )
    fetched = lax.all_to_all(served, "seq", split_axis=0, concat_axis=0, tiled=True)
    compact = take_blocks(owner_at, fetched)
    k1 = lax.all_gather(compact[:near], "head", axis=0, tiled=False)
    far_shape = (parts, places - near, BLOCK, width)
    k2 = lax.cond(
        overflow,
        lambda x: lax.all_gather(x, "head", axis=0, tiled=False),
        lambda x: jnp.zeros(far_shape, BF16),
        compact[near:],
    )
    out, d_queries, dk1, dk2 = attend(
        count[None], slots, q_pos % BLOCK, queries, d_out, k1, k2
    )
    r1 = lax.psum_scatter(dk1, "head", scatter_dimension=0, tiled=False)
    r2 = lax.cond(
        overflow,
        lambda x: lax.psum_scatter(x, "head", scatter_dimension=0, tiled=False),
        lambda x: jnp.zeros(far_shape[1:], BF16),
        dk2,
    )
    back = take_blocks(place_of, jnp.concatenate([r1, r2], axis=0))
    returned = lax.all_to_all(back, "seq", split_axis=0, concat_axis=0, tiled=True)
    owned = add_blocks(blocks_asked, returned, blocks_dev)
    d_cache = lax.psum_scatter(
        owned.reshape(blocks_dev * BLOCK, width), "head", scatter_dimension=0, tiled=True
    ).astype(F32)
    return (out, d_queries, d_cache)


def solution(mesh):
    placed = (
        P("seq", "head", None),
        P("seq", None),
        P("seq", "head", None),
        P("seq", None),
        P("seq"),
    )
    return jax.shard_map(
        on_device,
        mesh=mesh,
        in_specs=placed,
        out_specs=(P("seq", "head", None), P("seq", "head", None), P(("seq", "head"), None)),
        check_vma=False,
    )
```

time: 1460 us -> 365 us (0.25)
  matrix products: 574 us -> 0 us
  local copies, waits for them, and re-layouts: 489 us -> 37.5 us
  blocking collectives: 145 us -> 42 us
  Pallas kernels: 0 us -> 75.1 us
  other arithmetic: 36.4 us -> 11.6 us
  loops' own time: 15 us -> 0.01 us
    dot_general x66 -> x0, matrix products: 574 us -> none  [the longest x8 173 us: attend_batch(): jnp.dot(slot_onehot.astype(jnp.float32).T, key_terms, precision=lax.Preci...]
    reshape x22 -> x1, local copies, waits for them, and re-layouts: 312 us -> 4.45 us  [on_device(): owned.reshape(blocks_dev * BLOCK, width)]
    add x41 -> x0, local copies, waits for them, and re-layouts: 116 us -> none  [the longest x8 114 us: attend_rows(): d_key = d_key + jnp.concatenate([d_value, rope_zeros], axis=2)]
    all_to_all x1, blocking collectives: 145 us -> 42 us  [on_device(): lax.all_to_all(back, 'seq', split_axis=0, concat_axis=0, tiled=True)]
    all_to_all x1, waiting for transfers between devices: 134 us -> 31.3 us  [on_device(): lax.all_to_all(served, 'seq', split_axis=0, concat_axis=0, tiled=True)]
    pallas_call x0 -> x5, Pallas kernels: none -> 75.1 us  [the longest x1 60.3 us: attend(): pl.pallas_call(attend_kernel, out_shape=(jax.ShapeDtypeStruct((rows, head...]
    reduce_scatter x1 -> x2, waiting for transfers between devices: 23 us -> 82.4 us  [the longest x1 63.6 us: on_device(): r1 = lax.psum_scatter(dk1, 'head', scatter_dimension=0, tiled=False)]
    all_gather x0 -> x1, waiting for transfers between devices: none -> 48.8 us  [on_device(): k1 = lax.all_gather(compact[:near], 'head', axis=0, tiled=False)]
  transfers between devices with their start and end apart: 3 -> 5, of which waited for: 2 -> 5; matrix products, arithmetic and copies ran while one was open for 2% -> 7% of each run, Pallas kernels for 0% -> 0%
where the time goes in v1:
time: 365 us; the launch traced here: 364 us
  waiting for transfers between devices  166 us (45%)
  Pallas kernels  75.1 us (21%)
  blocking collectives  42 us (12%)
  local copies, waits for them, and re-layouts  37.5 us (10%)
  between operations  17 us (5%)
  starting transfers between devices  14.5 us (4%)
  other arithmetic  11.6 us (3%)
    reduce_scatter x1, waiting for transfers between devices, on_device(): r1 = lax.psum_scatter(dk1, 'head', scatter_dimension=0, tiled=False)  63.6 us
    pallas_call x1, Pallas kernels, attend(): pl.pallas_call(attend_kernel, out_shape=(jax.ShapeDtypeStruct((rows, head...  60.3 us
    all_gather x1, waiting for transfers between devices, on_device(): k1 = lax.all_gather(compact[:near], 'head', axis=0, tiled=False)  48.8 us
    all_to_all x1, blocking collectives, on_device(): lax.all_to_all(back, 'seq', split_axis=0, concat_axis=0, tiled=True)  42 us
    all_to_all x1, waiting for transfers between devices, on_device(): lax.all_to_all(served, 'seq', split_axis=0, concat_axis=0, tiled=True)  31.3 us
    unnamed x8, local copies, waits for them, and re-layouts  24.3 us
    reduce_scatter x1, waiting for transfers between devices, on_device(): lax.psum_scatter(owned.reshape(blocks_dev * BLOCK, width), 'head', scatte...  18.8 us
    pallas_call x3, Pallas kernels, take_blocks(): pl.pallas_call(take_blocks_kernel, out_shape=jax.ShapeDtypeStruct((count,...  10.6 us
  transfers between devices with their start and end apart: 5, of which 5 were waited for; matrix products, arithmetic and copies ran while one was open for 7% of the time, Pallas kernels for 0%

profile of v1, /device:TPU:1, one launch (start us, length us, event | category | flops | bytes accessed | tf_op | source)
XLA Modules:
  0.0 363.9 jit_solution(13428847968191989931)
XLA Ops:
  8.0 0.8 copy.24
  10.2 0.6 slice.27
  11.6 0.8 fusion.3
  12.3 0.7 copy.25
  13.0 9.6 %all-to-all-start = ((s32[32,1,2]{2,1,0:T(1,128)}), s32[32,1,2]{2,1,0:T(1,128)S(1)}, u32[]{:S(2)}, u32[]{:S(2)}) async-start(s32[32,1,2]{2,1,0:T(1,128)} %copy.25), calls=%async_computation.1 | async-start | bytes 32768 | tf_op jit(solution)/shard_map/all_to_all | solution.py:358
  22.6 4.3 %copy.27 = bf16[2048,576]{1,0:T(8,128)(2,1)} copy(bf16[2048,576]{0,1:T(8,128)(2,1)} %param.10) | data formatting | bytes 4718592 | tf_op args[1]
  27.0 2.5 all-to-all-done
  30.1 3.5 take_blocks.3
  33.6 4.9 %all-to-all-start.1 = ((bf16[32,64,576]{2,1,0:T(8,128)(2,1)}), bf16[32,64,576]{2,1,0:T(8,128)(2,1)S(1)}, u32[]{:S(2)}, u32[]{:S(2)}) async-start(bf16[32,64,576]{2,1,0:T(8,128)(2,1)} %take_blocks.3), calls=%async_computation.2 | async-start | bytes 5242880 | tf_op jit(solution)/shard_map/all_to_all | solution.py:365
  38.5 0.7 select_reduce_fusion.1.index_ref
  39.2 1.2 slice_bitcast_fusion
  41.1 31.3 %all-to-all-done.1.src = bf16[32,64,576]{2,1,0:T(8,128)(2,1)S(1)} async-done(((bf16[32,64,576]{2,1,0:T(8,128)(2,1)}), bf16[32,64,576]{2,1,0:T(8,128)(2,1)S(1)}, u32[]{:S(2)}, u32[]{:S(2)}) %all-to-all-start.1) | async-done | bytes 2359328 | tf_op jit(solution)/shard_map/all_to_all | solution.py:365
  72.4 1.5 copy-done
  73.9 3.5 take_blocks.4
  77.4 2.6 slice.32
  79.9 3.0 conditional.2
  79.9 3.0 broadcast.83
  83.5 9.0 %copy.28.q_hbm = bf16[128,32,576]{2,1,0:T(8,128)(2,1)} copy(bf16[128,32,576]{0,2,1:T(8,128)(2,1)} %param.9) | data formatting | bytes 9437184 | tf_op args[0]
  92.5 1.2 select_reduce_fusion.slot_ref
  94.3 48.8 %all-gather.7.cloned.1.call-done = bf16[68,64,576]{2,1,0:T(8,128)(2,1)} async-done(((bf16[17,64,576]{2,1,0:T(8,128)(2,1)}), bf16[68,64,576]{2,1,0:T(8,128)(2,1)}) %all-gather.7.cloned.1.call-update) | async-done | bytes 5013520 | tf_op jit(solution)/shard_map/all_gather | solution.py:367
  143.1 60.3 %attend.1 = (bf16[128,32,512]{2,1,0:T(8,128)(2,1)}, bf16[128,32,576]{2,1,0:T(8,128)(2,1)}, bf16[4,17,64,576]{3,2,1,0:T(8,128)(2,1)}, bf16[4,15,64,576]{3,2,1,0:T(8,128)(2,1)}) custom-call(s32[1]{0:T(128)} %add.51.count_ref, s32[768]{0:T(1024)} %select_reduce_fusion.slot_ref, s32[128]{0:T(128)} %and_select_fusion.limit_ref, ...), custom_call_target="tpu_custom_call" | custom-call | tf_op jit(solution)/shard_map/attend/pallas_call | solution.py:295
  203.3 1.2 conditional.3
  203.3 1.2 broadcast.84
  205.2 63.6 %reduce-scatter.6.cloned.1.call-done = bf16[1,17,64,576]{3,2,1,0:T(8,128)(2,1)} async-done(((bf16[4,17,64,576]{3,2,1,0:T(8,128)(2,1)}), bf16[1,17,64,576]{3,2,1,0:T(8,128)(2,1)}) %reduce-scatter.6.cloned.1.call-update) | async-done | bytes 1253392 | tf_op jit(solution)/shard_map/reduce_scatter | solution.py:378
  268.8 3.6 pad_maximum_fusion.src
  272.3 3.5 take_blocks.5
  275.9 42.0 %all_to_all.22.src = bf16[32,64,576]{2,1,0:T(8,128)(2,1)} all-to-all(bf16[32,64,576]{2,1,0:T(8,128)(2,1)} %take_blocks.5), channel_id=1, replica_groups=mesh['seq'=32,'head'=4] {'seq'}, dimensions={0} | all-to-all | bytes 4718592 | tf_op jit(solution)/shard_map/all_to_all | solution.py:386
  317.8 4.3 %add_blocks.1 = bf16[32,64,576]{2,1,0:T(8,128)(2,1)} custom-call(s32[32]{0:T(128)} %get-tuple-element.34.asked_ref, bf16[32,64,576]{2,1,0:T(8,128)(2,1)} %all_to_all.22.src), custom_call_target="tpu_custom_call" | custom-call | tf_op jit(solution)/shard_map/add_blocks/pallas_call | solution.py:76
  322.1 4.5 %copy.29 = bf16[2048,576]{0,1:T(8,128)(2,1)} copy(bf16[2048,576]{1,0:T(8,128)(2,1)} %bitcast.21) | data formatting | bytes 4718592 | tf_op jit(solution)/shard_map/reshape | solution.py:389
  326.6 8.7 %copy.30 = bf16[128,32,576]{0,2,1:T(8,128)(2,1)} copy(bf16[128,32,576]{2,1,0:T(8,128)(2,1)} %get-tuple-element.30) | data formatting | bytes 9437184
  335.3 18.8 %reduce-scatter.8.cloned.1.call-done = bf16[512,576]{0,1:T(8,128)(2,1)} async-done(((bf16[2048,576]{0,1:T(8,128)(2,1)}), bf16[512,576]{0,1:T(8,128)(2,1)}) %reduce-scatter.8.cloned.1.call-update) | async-done | bytes 589840 | tf_op jit(solution)/shard_map/reduce_scatter | solution.py:388
  354.1 2.2 convert_element_type.17
  (27 shorter events, 3.8 us)
Async XLA Ops:
  13.0 16.5 %all-to-all-start = ((s32[32,1,2]{2,1,0:T(1,128)}), s32[32,1,2]{2,1,0:T(1,128)S(1)}, u32[]{:S(2)}, u32[]{:S(2)}) async-start(s32[32,1,2]{2,1,0:T(1,128)} %copy.25), calls=%async_computation.1 | async-start | bytes 32768 | tf_op jit(solution)/shard_map/all_to_all | solution.py:358
  33.6 38.8 %all-to-all-start.1 = ((bf16[32,64,576]{2,1,0:T(8,128)(2,1)}), bf16[32,64,576]{2,1,0:T(8,128)(2,1)S(1)}, u32[]{:S(2)}, u32[]{:S(2)}) async-start(bf16[32,64,576]{2,1,0:T(8,128)(2,1)} %take_blocks.3), calls=%async_computation.2 | async-start | bytes 5242880 | tf_op jit(solution)/shard_map/all_to_all | solution.py:365
  72.4 1.5 copy-start
  83.0 60.1 %all-gather.7.cloned.1.call-start = ((), (), s32[]{:S(2)}) async-start(), calls=%async_computation.10 | async-start | bytes 6963200 | tf_op jit(solution)/shard_map/all_gather | solution.py:367
  83.5 10.2 %copy-start.1 = (s32[128]{0:T(128)S(1)}, s32[128]{0:T(128)}, u32[]{:S(2)}) copy-start(s32[128]{0:T(128)} %param.13) | copy-start | bytes 1540
  204.5 64.2 %reduce-scatter.6.cloned.1.call-start = ((), (), s32[]{:S(2)}) async-start(), calls=%async_computation.8 | async-start | bytes 6963200 | tf_op jit(solution)/shard_map/reduce_scatter | solution.py:378
  205.1 149.0 %reduce-scatter.8.cloned.1.call-start = ((), (), s32[]{:S(2)}) async-start(), calls=%async_computation.9 | async-start | bytes 2949120 | tf_op jit(solution)/shard_map/reduce_scatter | solution.py:388
Sparse Core Ops, SparseCore 1:
  85.8 57.2 all-gather.6
  207.5 61.2 reduce-scatter.5
  326.7 27.4 reduce-scatter.7

commit v2 on v1

--- a/solution.py
+++ b/solution.py
@@ -24,6 +24,8 @@
 SMEM = pl.BlockSpec(memory_space=pltpu.SMEM)
 VMEM = pl.BlockSpec(memory_space=pltpu.VMEM)
 VMEM_BYTES = 60 * 2**20
+CHUNKS = 4
+MESH = pl.DeviceIdType.MESH
 
 
 def take_blocks_kernel(index_ref, src, dst, sems):
@@ -55,6 +57,140 @@
     )(index, blocks)
 
 
+def unset_kernel(after_ref, out):
+    del after_ref, out
+
+
+def unset(after, shape):
+    return pl.pallas_call(
+        unset_kernel,
+        out_shape=jax.ShapeDtypeStruct(shape, BF16),
+        in_specs=[HBM],
+        out_specs=HBM,
+        name="unset",
+    )(after)
+
+
+def fetch_kernel(asked_ref, owner_ref, cache_v, near_hbm, all_hbm,
+                 send_v, recv, pack_v, a_send, a_recv, x_send, x_recv, own_sem, all_sem):
+    chunks, seq_count, rows, _ = send_v.shape
+    near = pack_v.shape[1]
+    parts = near_hbm.shape[1]
+    cut = (near + 1) // 2
+    me, part = lax.axis_index("seq"), lax.axis_index("head")
+    right, left = lax.rem(part + 1, parts), lax.rem(part + parts - 1, parts)
+    barrier = pltpu.get_barrier_semaphore()
+
+    def greet(d, c):
+        peer = lax.rem(me + d, seq_count)
+        pl.semaphore_signal(barrier, inc=1, device_id=(peer, part), device_id_type=MESH)
+        return c
+
+    lax.fori_loop(1, seq_count, greet, 0)
+    for x in (left, right):
+        pl.semaphore_signal(barrier, inc=1, device_id=(me, x), device_id_type=MESH)
+    for c in range(chunks):
+
+        def serve(p, x, c=c):
+            send_v[c, p] = cache_v[asked_ref[p], c * rows : (c + 1) * rows]
+            return x
+
+        lax.fori_loop(0, seq_count, serve, 0)
+    pl.semaphore_wait(barrier, seq_count + 1)
+    for c in range(chunks):
+
+        def send(d, x, c=c):
+            peer = lax.rem(me + d, seq_count)
+            pltpu.make_async_remote_copy(
+                src_ref=send_v.at[c, peer], dst_ref=recv[c].at[me],
+                send_sem=a_send.at[c], recv_sem=a_recv.at[c],
+                device_id=(peer, part), device_id_type=MESH,
+            ).start()
+            return x
+
+        lax.fori_loop(1, seq_count, send, 0)
+        recv[c][me] = send_v[c, me]
+
+    def over_x(c, way, src, dst, to):
+        return pltpu.make_async_remote_copy(
+            src_ref=src, dst_ref=dst, send_sem=x_send.at[c, way], recv_sem=x_recv.at[c, way],
+            device_id=(me, to), device_id_type=MESH,
+        )
+
+    def direct(c):
+        out = near_hbm.at[c, part]
+        return (over_x(c, 0, pack_v.at[c], out, right), over_x(c, 1, pack_v.at[c], out, left))
+
+    def onward(c):
+        one = near_hbm.at[c, left, pl.ds(0, cut)]
+        two = near_hbm.at[c, right, pl.ds(cut, near - cut)]
+        return (over_x(c, 2, one, one, right), over_x(c, 3, two, two, left))
+
+    def own(c):
+        return pltpu.make_async_copy(pack_v.at[c], near_hbm.at[c, part], own_sem.at[c])
+
+    def keep(c):
+        return pltpu.make_async_copy(recv[c], all_hbm.at[c], all_sem.at[c])
+
+    def forward(c):
+        for x, y in zip(direct(c), onward(c)):
+            x.wait_recv()
+            y.start()
+
+    for c in range(chunks):
+        whole = recv[c].at[pl.ds(0, seq_count - 1)]
+        pltpu.make_async_copy(whole, whole, a_recv.at[c]).wait()
+
+        def pack(i, x, c=c):
+            pack_v[c, i] = recv[c][owner_ref[i]]
+            return x
+
+        lax.fori_loop(0, near, pack, 0)
+        for x in direct(c):
+            x.start()
+        own(c).start()
+        keep(c).start()
+        if c:
+            forward(c - 1)
+    forward(chunks - 1)
+    for c in range(chunks):
+        whole = send_v.at[c, pl.ds(0, seq_count - 1)]
+        pltpu.make_async_copy(whole, whole, a_send.at[c]).wait()
+        own(c).wait()
+        keep(c).wait()
+        for x, y in zip(direct(c), onward(c)):
+            x.wait_send()
+            y.wait_send()
+            y.wait_recv()
+
+
+def fetch(asked, owner_at, blocks, near, parts):
+    seq_count = asked.shape[0]
+    width = blocks.shape[2]
+    rows = BLOCK // CHUNKS
+    dma = pltpu.SemaphoreType.DMA
+    return pl.pallas_call(
+        fetch_kernel,
+        out_shape=(
+            jax.ShapeDtypeStruct((CHUNKS, parts, near, rows, width), BF16),
+            jax.ShapeDtypeStruct((CHUNKS, seq_count, rows, width), BF16),
+        ),
+        in_specs=[SMEM, SMEM, VMEM],
+        out_specs=(HBM, HBM),
+        scratch_shapes=[
+            pltpu.VMEM((CHUNKS, seq_count, rows, width), BF16),
+            [pltpu.VMEM((seq_count, rows, width), BF16)] * CHUNKS,
+            pltpu.VMEM((CHUNKS, near, rows, width), BF16),
+            dma((CHUNKS,)), dma((CHUNKS,)), dma((CHUNKS, 4)), dma((CHUNKS, 4)),
+            dma((CHUNKS,)), dma((CHUNKS,)),
+        ],
+        compiler_params=pltpu.CompilerParams(
+            vmem_limit_bytes=VMEM_BYTES, collective_id=1, has_side_effects=True
+        ),
+        name="fetch",
+    )(asked, owner_at, blocks)
+
+
 def add_blocks_kernel(asked_ref, src, out, total):
     total[...] = jnp.zeros_like(total)
 
@@ -93,7 +229,7 @@
     rows, heads, width = q_v.shape
     lat = g_v.shape[2]
     parts, places = k_v.shape[0], k_v.shape[1]
-    near = k1_hbm.shape[1]
+    chunks, _, near, piece, _ = k1_hbm.shape
     groups = rows // COPY_ROWS
     slots = parts * places
     more = count_ref[0] > parts * near
@@ -114,12 +250,15 @@
         )
 
     key_copies = [
-        pltpu.make_async_copy(k1_hbm.at[h], k_v.at[h, pl.ds(0, near)], sem_k.at[h])
+        pltpu.make_async_copy(
+            k1_hbm.at[c, h], k_v.at[h, pl.ds(0, near), pl.ds(c * piece, piece)], sem_k.at[c, h]
+        )
+        for c in range(chunks)
         for h in range(parts)
     ]
     far_copies = [
         pltpu.make_async_copy(
-            k2_hbm.at[h], k_v.at[h, pl.ds(near, places - near)], sem_k.at[parts + h]
+            k2_hbm.at[h], k_v.at[h, pl.ds(near, places - near)], sem_k.at[chunks, h]
         )
         for h in range(parts)
     ]
@@ -289,7 +428,7 @@
 def attend(count, slots, limit, queries, d_out, k1, k2):
     rows, heads, width = queries.shape
     lat = d_out.shape[2]
-    parts, near = k1.shape[:2]
+    parts, near = k1.shape[1:3]
     places = near + k2.shape[1]
     groups = rows // COPY_ROWS
     return pl.pallas_call(
@@ -297,7 +436,7 @@
         out_shape=(
             jax.ShapeDtypeStruct((rows, heads, lat), BF16),
             jax.ShapeDtypeStruct((rows, heads, width), BF16),
-            jax.ShapeDtypeStruct(k1.shape, BF16),
+            jax.ShapeDtypeStruct((parts, near, BLOCK, width), BF16),
             jax.ShapeDtypeStruct(k2.shape, BF16),
         ),
         in_specs=[SMEM, SMEM, SMEM, HBM, HBM, HBM, HBM],
@@ -315,7 +454,7 @@
             pltpu.SMEM((parts * places,), jnp.int32),
             pltpu.SMEM((parts * places * rows,), jnp.int32),
             pltpu.SemaphoreType.DMA((groups, 2)),
-            pltpu.SemaphoreType.DMA((2 * parts,)),
+            pltpu.SemaphoreType.DMA((CHUNKS + 1, parts)),
             pltpu.SemaphoreType.DMA((2, 2)),
             pltpu.SemaphoreType.DMA((2,)),
         ],
@@ -359,19 +498,20 @@
     blocks_asked = asked[:, 0]
     overflow = jnp.max(asked[:, 1]) > near * parts
 
-    served = take_blocks(
-        jnp.maximum(blocks_asked, 0), cache.reshape(blocks_dev, BLOCK, width)
-    )
-    fetched = lax.all_to_all(served, "seq", split_axis=0, concat_axis=0, tiled=True)
-    compact = take_blocks(owner_at, fetched)
-    k1 = lax.all_gather(compact[:near], "head", axis=0, tiled=False)
+    k1, fetched = fetch(
+        jnp.maximum(blocks_asked, 0),
+        owner_at[:near],
+        cache.reshape(blocks_dev, BLOCK, width),
+        near,
+        parts,
+    )
     far_shape = (parts, places - near, BLOCK, width)
-    k2 = lax.cond(
-        overflow,
-        lambda x: lax.all_gather(x, "head", axis=0, tiled=False),
-        lambda x: jnp.zeros(far_shape, BF16),
-        compact[near:],
-    )
+
+    def gather_far(x):
+        x = x.transpose(1, 0, 2, 3).reshape(seq_count, BLOCK, width)
+        return lax.all_gather(take_blocks(owner_at[near:], x), "head", axis=0, tiled=False)
+
+    k2 = lax.cond(overflow, gather_far, lambda x: unset(x, far_shape), fetched)
     out, d_queries, dk1, dk2 = attend(
         count[None], slots, q_pos % BLOCK, queries, d_out, k1, k2
     )
@@ -379,7 +519,7 @@
     r2 = lax.cond(
         overflow,
         lambda x: lax.psum_scatter(x, "head", scatter_dimension=0, tiled=False),
-        lambda x: jnp.zeros(far_shape[1:], BF16),
+        lambda x: unset(x, far_shape[1:]),
         dk2,
     )
     back = take_blocks(place_of, jnp.concatenate([r1, r2], axis=0))

time: 365 us -> 334 us (0.915)
  waiting for transfers between devices: 166 us -> 86.2 us
  Pallas kernels: 75.1 us -> 137 us
  local copies, waits for them, and re-layouts: 37.5 us -> 29.3 us
  starting transfers between devices: 14.5 us -> 9.69 us
    pallas_call x0 -> x3, Pallas kernels: none -> 68 us  [the longest x1 68 us: fetch(): pl.pallas_call(fetch_kernel, out_shape=(jax.ShapeDtypeStruct((CHUNKS, par...]
    all_gather x1 -> x0, waiting for transfers between devices: 48.8 us -> none  [on_device(): k1 = lax.all_gather(compact[:near], 'head', axis=0, tiled=False)]
    all_to_all x1 -> x0, waiting for transfers between devices: 31.3 us -> none  [on_device(): lax.all_to_all(served, 'seq', split_axis=0, concat_axis=0, tiled=True)]
    pallas_call x3 -> x1, Pallas kernels: 10.6 us -> 3.54 us  [take_blocks(): pl.pallas_call(take_blocks_kernel, out_shape=jax.ShapeDtypeStruct((count,...]
    all_to_all x1 -> x0, starting transfers between devices: 4.86 us -> none  [on_device(): lax.all_to_all(served, 'seq', split_axis=0, concat_axis=0, tiled=True)]
    another operation x7 -> x4, local copies, waits for them, and re-layouts: 4.63 us -> 0.34 us
    unnamed x8 -> x4, local copies, waits for them, and re-layouts: 24.3 us -> 22.8 us
  transfers between devices with their start and end apart: 5 -> 3, of which waited for: 5 -> 2; matrix products, arithmetic and copies ran while one was open for 7% -> 7% of each run, Pallas kernels for 0% -> 0%
where the time goes in v2:
time: 334 us; the launch traced here: 333 us
  Pallas kernels  137 us (41%)
  waiting for transfers between devices  86.2 us (26%)
  blocking collectives  42 us (13%)
  local copies, waits for them, and re-layouts  29.3 us (9%)
  between operations  16.9 us (5%)
  other arithmetic  11.9 us (4%)
  starting transfers between devices  9.69 us (3%)
    pallas_call x1, Pallas kernels, fetch(): pl.pallas_call(fetch_kernel, out_shape=(jax.ShapeDtypeStruct((CHUNKS, par...  68 us
    reduce_scatter x1, waiting for transfers between devices, on_device(): r1 = lax.psum_scatter(dk1, 'head', scatter_dimension=0, tiled=False)  67 us
    pallas_call x1, Pallas kernels, attend(): pl.pallas_call(attend_kernel, out_shape=(jax.ShapeDtypeStruct((rows, head...  60.8 us
    all_to_all x1, blocking collectives, on_device(): lax.all_to_all(back, 'seq', split_axis=0, concat_axis=0, tiled=True)  42 us
    unnamed x4, local copies, waits for them, and re-layouts  22.8 us
    reduce_scatter x1, waiting for transfers between devices, on_device(): lax.psum_scatter(owned.reshape(blocks_dev * BLOCK, width), 'head', scatte...  18.7 us
    all_to_all x1, starting transfers between devices, on_device(): lax.all_to_all(request, 'seq', split_axis=0, concat_axis=0, tiled=True)  9.61 us
  transfers between devices with their start and end apart: 3, of which 2 were waited for; matrix products, arithmetic and copies ran while one was open for 7% of the time, Pallas kernels for 0%

profile of v2, /device:TPU:1, one launch (start us, length us, event | category | flops | bytes accessed | tf_op | source)
XLA Modules:
  0.0 332.6 jit_solution(17922865418331283090)
XLA Ops:
  8.0 0.8 copy.27
  8.8 0.1 eq.39
  8.9 0.5 fusion
  9.4 0.1 reduce_or.12
  9.5 0.3 reduce-window.9
  9.8 0.1 slice.22
  10.0 0.1 slice_reduce_fusion
  10.2 0.6 slice.24
  10.8 0.1 reshape.82
  11.6 0.8 fusion.3
  12.3 0.7 copy.28
  13.0 9.6 %all-to-all-start = ((s32[32,1,2]{2,1,0:T(1,128)}), s32[32,1,2]{2,1,0:T(1,128)S(1)}, u32[]{:S(2)}, u32[]{:S(2)}) async-start(s32[32,1,2]{2,1,0:T(1,128)} %copy.28), calls=%async_computation.1 | async-start | bytes 32768 | tf_op jit(solution)/shard_map/all_to_all | solution.py:497
  22.7 1.2 select_reduce_fusion.slot_ref
  23.9 1.2 and_select_fusion.limit_ref
  25.1 0.2 select_reduce_fusion.1
  25.3 4.3 %copy.30 = bf16[2048,576]{1,0:T(8,128)(2,1)} copy(bf16[2048,576]{0,1:T(8,128)(2,1)} %param.10) | data formatting | bytes 4718592 | tf_op args[1]
  29.7 9.0 %copy.32.q_hbm = bf16[128,32,576]{2,1,0:T(8,128)(2,1)} copy(bf16[128,32,576]{0,2,1:T(8,128)(2,1)} %param.9) | data formatting | bytes 9437184 | tf_op args[0]
  38.7 0.1 copy.29
  38.7 0.5 broadcast_maximum_fusion.asked_ref
  39.2 1.2 slice_bitcast_fusion
  41.1 68.0 %fetch.1 = (bf16[4,4,17,16,576]{4,3,2,1,0:T(8,128)(2,1)}, bf16[4,32,16,576]{3,2,1,0:T(8,128)(2,1)S(1)}) custom-call(s32[32]{0:T(128)} %broadcast_maximum_fusion.asked_ref, s32[17]{0:T(128)S(1)} %bitcast.29, bf16[32,64,576]{2,1,0:T(8,128)(2,1)} %bitcast.23), custom_call_target="tpu_custom_call" | custom-call | tf_op jit(solution)/shard_map/fetch/pallas_call | solution.py:172
  109.2 60.8 %attend.1 = (bf16[128,32,512]{2,1,0:T(8,128)(2,1)}, bf16[128,32,576]{2,1,0:T(8,128)(2,1)}, bf16[4,17,64,576]{3,2,1,0:T(8,128)(2,1)}, bf16[4,15,64,576]{3,2,1,0:T(8,128)(2,1)}) custom-call(s32[1]{0:T(128)} %add.51.count_ref, s32[768]{0:T(1024)} %select_reduce_fusion.slot_ref, s32[128]{0:T(128)} %and_select_fusion.limit_ref, ...), custom_call_target="tpu_custom_call" | custom-call | tf_op jit(solution)/shard_map/attend/pallas_call | solution.py:434
  170.1 0.5 reduce-scatter.6.cloned.1.call-update
  170.7 67.0 %reduce-scatter.6.cloned.1.call-done = bf16[1,17,64,576]{3,2,1,0:T(8,128)(2,1)} async-done(((bf16[4,17,64,576]{3,2,1,0:T(8,128)(2,1)}), bf16[1,17,64,576]{3,2,1,0:T(8,128)(2,1)}) %reduce-scatter.6.cloned.1.call-update) | async-done | bytes 1253392 | tf_op jit(solution)/shard_map/reduce_scatter | solution.py:518
  237.7 3.6 %pad_maximum_fusion.src = bf16[32,64,576]{2,1,0:T(8,128)(2,1)} fusion(bf16[15,64,576]{2,1,0:T(8,128)(2,1)} %get-tuple-element.55, bf16[17,64,576]{2,1,0:T(8,128)(2,1)} %bitcast.26), kind=kLoop, calls=%fused_computation.3 | loop fusion | flops 1179648 | bytes 4718592 | tf_op jit(solution)/shard_map/concatenate | solution.py:525
  241.2 3.5 %take_blocks.3 = bf16[32,64,576]{2,1,0:T(8,128)(2,1)} custom-call(s32[32]{0:T(128)} %get-tuple-element.50.index_ref, bf16[32,64,576]{2,1,0:T(8,128)(2,1)} %pad_maximum_fusion.src), custom_call_target="tpu_custom_call" | custom-call | tf_op jit(solution)/shard_map/take_blocks/pallas_call | solution.py:49
  244.8 42.0 %all_to_all.17.src = bf16[32,64,576]{2,1,0:T(8,128)(2,1)} all-to-all(bf16[32,64,576]{2,1,0:T(8,128)(2,1)} %take_blocks.3), channel_id=1, replica_groups=mesh['seq'=32,'head'=4] {'seq'}, dimensions={0} | all-to-all | bytes 4718592 | tf_op jit(solution)/shard_map/all_to_all | solution.py:526
  286.7 4.3 %add_blocks.1 = bf16[32,64,576]{2,1,0:T(8,128)(2,1)} custom-call(s32[32]{0:T(128)} %get-tuple-element.52.asked_ref, bf16[32,64,576]{2,1,0:T(8,128)(2,1)} %all_to_all.17.src), custom_call_target="tpu_custom_call" | custom-call | tf_op jit(solution)/shard_map/add_blocks/pallas_call | solution.py:212
  291.0 4.5 %copy.33 = bf16[2048,576]{0,1:T(8,128)(2,1)} copy(bf16[2048,576]{1,0:T(8,128)(2,1)} %bitcast.24) | data formatting | bytes 4718592 | tf_op jit(solution)/shard_map/reshape | solution.py:529
  295.5 8.7 %copy.34 = bf16[128,32,576]{0,2,1:T(8,128)(2,1)} copy(bf16[128,32,576]{2,1,0:T(8,128)(2,1)} %get-tuple-element.48) | data formatting | bytes 9437184
  304.2 18.7 %reduce-scatter.8.cloned.1.call-done = bf16[512,576]{0,1:T(8,128)(2,1)} async-done(((bf16[2048,576]{0,1:T(8,128)(2,1)}), bf16[512,576]{0,1:T(8,128)(2,1)}) %reduce-scatter.8.cloned.1.call-update) | async-done | bytes 589840 | tf_op jit(solution)/shard_map/reduce_scatter | solution.py:528
  322.9 2.2 convert_element_type.17
  (16 shorter events, 0.4 us)
Async XLA Ops:
  13.0 25.6 %all-to-all-start = ((s32[32,1,2]{2,1,0:T(1,128)}), s32[32,1,2]{2,1,0:T(1,128)S(1)}, u32[]{:S(2)}, u32[]{:S(2)}) async-start(s32[32,1,2]{2,1,0:T(1,128)} %copy.28), calls=%async_computation.1 | async-start | bytes 32768 | tf_op jit(solution)/shard_map/all_to_all | solution.py:497
  170.0 67.6 %reduce-scatter.6.cloned.1.call-start = ((), (), s32[]{:S(2)}) async-start(), calls=%async_computation.7 | async-start | bytes 6963200 | tf_op jit(solution)/shard_map/reduce_scatter | solution.py:518
  170.6 152.3 %reduce-scatter.8.cloned.1.call-start = ((), (), s32[]{:S(2)}) async-start(), calls=%async_computation.8 | async-start | bytes 2949120 | tf_op jit(solution)/shard_map/reduce_scatter | solution.py:528
Sparse Core Ops, SparseCore 1:
  173.1 64.5 reduce-scatter.5
  295.6 27.3 reduce-scatter.7

commit v3 on v2

--- a/solution.py
+++ b/solution.py
@@ -25,6 +25,7 @@
 VMEM = pl.BlockSpec(memory_space=pltpu.VMEM)
 VMEM_BYTES = 60 * 2**20
 CHUNKS = 4
+STRIDE = 13
 MESH = pl.DeviceIdType.MESH
 
 
@@ -82,7 +83,7 @@
     barrier = pltpu.get_barrier_semaphore()
 
     def greet(d, c):
-        peer = lax.rem(me + d, seq_count)
+        peer = lax.rem(me + d * STRIDE, seq_count)
         pl.semaphore_signal(barrier, inc=1, device_id=(peer, part), device_id_type=MESH)
         return c
 
@@ -100,7 +101,7 @@
     for c in range(chunks):
 
         def send(d, x, c=c):
-            peer = lax.rem(me + d, seq_count)
+            peer = lax.rem(me + d * STRIDE, seq_count)
             pltpu.make_async_remote_copy(
                 src_ref=send_v.at[c, peer], dst_ref=recv[c].at[me],
                 send_sem=a_send.at[c], recv_sem=a_recv.at[c],
@@ -191,24 +192,153 @@
     )(asked, owner_at, blocks)
 
 
+def give_back_kernel(place_ref, dk_v, far_v, out_hbm,
+                     sum_r, sum_l, one_l, one_r, two_l, two_r, places_v, back_v,
+                     x_send, x_recv, a_send, a_recv, own_sem):
+    chunks, parts, near, rows, _ = dk_v.shape
+    seq_count = back_v.shape[1]
+    cut = (near + 1) // 2
+    me, part = lax.axis_index("seq"), lax.axis_index("head")
+    right, left = lax.rem(part + 1, parts), lax.rem(part + parts - 1, parts)
+    far = lax.rem(part + 2, parts)
+    barrier = pltpu.get_barrier_semaphore()
+
+    def greet(d, c):
+        peer = lax.rem(me + d * STRIDE, seq_count)
+        pl.semaphore_signal(barrier, inc=1, device_id=(peer, part), device_id_type=MESH)
+        return c
+
+    lax.fori_loop(1, seq_count, greet, 0)
+    for x in (left, right):
+        pl.semaphore_signal(barrier, inc=1, device_id=(me, x), device_id_type=MESH)
+    pl.semaphore_wait(barrier, seq_count + 1)
+
+    def over_x(c, way, src, dst, to):
+        return pltpu.make_async_remote_copy(
+            src_ref=src, dst_ref=dst, send_sem=x_send.at[c, way], recv_sem=x_recv.at[c, way],
+            device_id=(me, to), device_id_type=MESH,
+        )
+
+    def first(c):
+        return (
+            over_x(c, 0, dk_v.at[c, far, pl.ds(0, cut)], one_l.at[c], right),
+            over_x(c, 1, dk_v.at[c, far, pl.ds(cut, near - cut)], one_r.at[c], left),
+        )
+
+    def second(c):
+        return (
+            over_x(c, 2, sum_r.at[c], two_l.at[c], right),
+            over_x(c, 3, sum_l.at[c], two_r.at[c], left),
+        )
+
+    def own(c):
+        return pltpu.make_async_copy(back_v.at[c, me], out_hbm.at[c, me], own_sem.at[c])
+
+    def begin(c):
+        for x in first(c):
+            x.start()
+
+    def add_far(c):
+        from_left, from_right = first(c)
+        to_right, to_left = second(c)
+        from_left.wait_recv()
+        sum_r[c, :cut] = (dk_v[c, right, :cut].astype(F32) + one_l[c].astype(F32)).astype(BF16)
+        sum_r[c, cut:] = dk_v[c, right, cut:]
+        to_right.start()
+        from_right.wait_recv()
+        sum_l[c, :cut] = dk_v[c, left, :cut]
+        sum_l[c, cut:] = (dk_v[c, left, cut:].astype(F32) + one_r[c].astype(F32)).astype(BF16)
+        to_left.start()
+
+    def to_owners(c):
+        for x in second(c):
+            x.wait_recv()
+        places_v[:near] = (
+            dk_v[c, part].astype(F32) + two_l[c].astype(F32) + two_r[c].astype(F32)
+        ).astype(BF16)
+        places_v[near:] = far_v[:, c * rows : (c + 1) * rows]
+
+        def place(o, x):
+            back_v[c, o] = places_v[place_ref[o]]
+            return x
+
+        lax.fori_loop(0, seq_count, place, 0)
+
+        def send(d, x):
+            peer = lax.rem(me + d * STRIDE, seq_count)
+            pltpu.make_async_remote_copy(
+                src_ref=back_v.at[c, peer], dst_ref=out_hbm.at[c, me],
+                send_sem=a_send.at[c], recv_sem=a_recv.at[c],
+                device_id=(peer, part), device_id_type=MESH,
+            ).start()
+            return x
+
+        lax.fori_loop(1, seq_count, send, 0)
+        own(c).start()
+
+    begin(0)
+    begin(1)
+    for c in range(chunks + 1):
+        if c < chunks:
+            add_far(c)
+        if c + 2 < chunks:
+            begin(c + 2)
+        if c:
+            to_owners(c - 1)
+    for c in range(chunks):
+        whole = back_v.at[c, pl.ds(0, seq_count - 1)]
+        pltpu.make_async_copy(whole, whole, a_send.at[c]).wait()
+        landed = out_hbm.at[c, pl.ds(0, seq_count - 1)]
+        pltpu.make_async_copy(landed, landed, a_recv.at[c]).wait()
+        own(c).wait()
+        for x in first(c) + second(c):
+            x.wait_send()
+
+
+def give_back(place_of, dk, far):
+    chunks, parts, near, rows, width = dk.shape
+    seq_count = place_of.shape[0]
+    cut = (near + 1) // 2
+    dma = pltpu.SemaphoreType.DMA
+    piece = [pltpu.VMEM((chunks, n, rows, width), BF16)
+             for n in (near, near, cut, near - cut, near, near)]
+    return pl.pallas_call(
+        give_back_kernel,
+        out_shape=jax.ShapeDtypeStruct((chunks, seq_count, rows, width), BF16),
+        in_specs=[SMEM, VMEM, VMEM],
+        out_specs=HBM,
+        scratch_shapes=piece + [
+            pltpu.VMEM((near + far.shape[0], rows, width), BF16),
+            pltpu.VMEM((chunks, seq_count, rows, width), BF16),
+            dma((chunks, 4)), dma((chunks, 4)), dma((chunks,)), dma((chunks,)), dma((chunks,)),
+        ],
+        compiler_params=pltpu.CompilerParams(
+            vmem_limit_bytes=VMEM_BYTES, collective_id=2, has_side_effects=True
+        ),
+        name="give_back",
+    )(place_of, dk, far)
+
+
 def add_blocks_kernel(asked_ref, src, out, total):
+    chunks, seq_count, rows, _ = src.shape
     total[...] = jnp.zeros_like(total)
 
-    def add(i, c):
+    def add(i, x):
         block = asked_ref[i]
 
         @pl.when(block >= 0)
         def _():
-            total[block] += src[i].astype(F32)
-
-        return c
-
-    lax.fori_loop(0, src.shape[0], add, 0)
+            for c in range(chunks):
+                total[block, c * rows : (c + 1) * rows] += src[c, i].astype(F32)
+
+        return x
+
+    lax.fori_loop(0, seq_count, add, 0)
     out[...] = total[...].astype(out.dtype)
 
 
 def add_blocks(asked, returned, blocks_dev):
-    shape = (blocks_dev,) + returned.shape[1:]
+    shape = (blocks_dev, BLOCK, returned.shape[-1])
     return pl.pallas_call(
         add_blocks_kernel,
         out_shape=jax.ShapeDtypeStruct(shape, BF16),
@@ -394,31 +524,43 @@
 
         lax.fori_loop(1, (most + CHUNK - 1) // CHUNK, again, 0)
 
-    def key_loop(begin, end, dk_hbm):
-        def dk_copy(place):
-            b = lax.rem(place, 2)
-            return pltpu.make_async_copy(dk_v.at[b], dk_hbm.at[:, place - begin], sem_dk.at[b])
-
+    def near_copies(place):
+        b = lax.rem(place, 2)
+        return [
+            pltpu.make_async_copy(
+                dk_v.at[b, :, pl.ds(c * piece, piece)], dk1_hbm.at[c, :, place], sem_dk.at[b, c]
+            )
+            for c in range(chunks)
+        ]
+
+    def far_copies_out(place):
+        b = lax.rem(place, 2)
+        return [pltpu.make_async_copy(dk_v.at[b], dk2_hbm.at[:, place - near], sem_dk.at[b, 0])]
+
+    def key_loop(begin, end, copies):
         def body(place, c):
             key_step(place)
 
             @pl.when(place >= begin + 2)
             def _():
-                dk_copy(place - 2).wait()
+                for x in copies(place - 2):
+                    x.wait()
 
             dk_v[lax.rem(place, 2)] = acc_v[...].astype(BF16)
-            dk_copy(place).start()
+            for x in copies(place):
+                x.start()
             return c
 
         lax.fori_loop(begin, end, body, 0)
-        dk_copy(jnp.int32(end - 2)).wait()
-        dk_copy(jnp.int32(end - 1)).wait()
-
-    key_loop(0, near, dk1_hbm)
+        for place in (end - 2, end - 1):
+            for x in copies(jnp.int32(place)):
+                x.wait()
+
+    key_loop(0, near, near_copies)
 
     @pl.when(more)
     def _():
-        key_loop(near, places, dk2_hbm)
+        key_loop(near, places, far_copies_out)
 
     for i in (groups - 2, groups - 1):
         for c in out_copies(jnp.int32(i)):
@@ -436,7 +578,7 @@
         out_shape=(
             jax.ShapeDtypeStruct((rows, heads, lat), BF16),
             jax.ShapeDtypeStruct((rows, heads, width), BF16),
-            jax.ShapeDtypeStruct((parts, near, BLOCK, width), BF16),
+            jax.ShapeDtypeStruct(k1.shape, BF16),
             jax.ShapeDtypeStruct(k2.shape, BF16),
         ),
         in_specs=[SMEM, SMEM, SMEM, HBM, HBM, HBM, HBM],
@@ -456,11 +598,26 @@
             pltpu.SemaphoreType.DMA((groups, 2)),
             pltpu.SemaphoreType.DMA((CHUNKS + 1, parts)),
             pltpu.SemaphoreType.DMA((2, 2)),
-            pltpu.SemaphoreType.DMA((2,)),
+            pltpu.SemaphoreType.DMA((2, CHUNKS)),
         ],
         compiler_params=pltpu.CompilerParams(vmem_limit_bytes=VMEM_BYTES),
         name="attend",
     )(count, slots, limit, queries, d_out, k1, k2)
+
+
+def turn_kernel(src, out):
+    out[...] = src[...].astype(F32).T
+
+
+def widen_turned(rows):
+    return pl.pallas_call(
+        turn_kernel,
+        out_shape=jax.ShapeDtypeStruct(rows.shape[::-1], F32),
+        in_specs=[VMEM],
+        out_specs=VMEM,
+        compiler_params=pltpu.CompilerParams(vmem_limit_bytes=VMEM_BYTES),
+        name="widen_turned",
+    )(rows).T
 
 
 def on_device(queries, cache, d_out, picks, q_pos):
@@ -515,19 +672,19 @@
     out, d_queries, dk1, dk2 = attend(
         count[None], slots, q_pos % BLOCK, queries, d_out, k1, k2
     )
-    r1 = lax.psum_scatter(dk1, "head", scatter_dimension=0, tiled=False)
     r2 = lax.cond(
         overflow,
         lambda x: lax.psum_scatter(x, "head", scatter_dimension=0, tiled=False),
         lambda x: unset(x, far_shape[1:]),
         dk2,
     )
-    back = take_blocks(place_of, jnp.concatenate([r1, r2], axis=0))
-    returned = lax.all_to_all(back, "seq", split_axis=0, concat_axis=0, tiled=True)
+    returned = give_back(place_of, dk1, r2)
     owned = add_blocks(blocks_asked, returned, blocks_dev)
-    d_cache = lax.psum_scatter(
-        owned.reshape(blocks_dev * BLOCK, width), "head", scatter_dimension=0, tiled=True
-    ).astype(F32)
+    d_cache = widen_turned(
+        lax.psum_scatter(
+            owned.reshape(blocks_dev * BLOCK, width), "head", scatter_dimension=0, tiled=True
+        )
+    )
     return (out, d_queries, d_cache)
 
 

time: 334 us -> 282 us (0.84)
  Pallas kernels: 137 us -> 203 us
  waiting for transfers between devices: 86.2 us -> 21.8 us
  blocking collectives: 42 us -> 0 us
  other arithmetic: 11.9 us -> 6.08 us
  local copies, waits for them, and re-layouts: 29.3 us -> 24.7 us
    reduce_scatter x1 -> x0, waiting for transfers between devices: 67 us -> none  [on_device(): r1 = lax.psum_scatter(dk1, 'head', scatter_dimension=0, tiled=False)]
    pallas_call x1 -> x2, Pallas kernels: 3.54 us -> 70 us  [the longest x1 67.7 us: give_back(): pl.pallas_call(give_back_kernel, out_shape=jax.ShapeDtypeStruct((chunks,...]
    all_to_all x1 -> x0, blocking collectives: 42 us -> none  [on_device(): lax.all_to_all(back, 'seq', split_axis=0, concat_axis=0, tiled=True)]
    reshape x1 -> x0, local copies, waits for them, and re-layouts: 4.45 us -> none  [on_device(): owned.reshape(blocks_dev * BLOCK, width)]
    concatenate x1 -> x0, other arithmetic: 3.57 us -> none  [on_device(): back = take_blocks(place_of, jnp.concatenate([r1, r2], axis=0))]
  transfers between devices with their start and end apart: 3 -> 2, of which waited for: 2 -> 1; matrix products, arithmetic and copies ran while one was open for 7% -> 9% of each run, Pallas kernels for 0% -> 0%
where the time goes in v3:
time: 282 us
  Pallas kernels  203 us (72%)
  local copies, waits for them, and re-layouts  24.7 us (9%)
  waiting for transfers between devices  21.8 us (8%)
  between operations  16.8 us (6%)
  starting transfers between devices  9.65 us (3%)
  other arithmetic  6.08 us (2%)
    pallas_call x1, Pallas kernels, give_back(): pl.pallas_call(give_back_kernel, out_shape=jax.ShapeDtypeStruct((chunks,...  67.7 us
    pallas_call x1, Pallas kernels, fetch(): pl.pallas_call(fetch_kernel, out_shape=(jax.ShapeDtypeStruct((CHUNKS, par...  67 us
    pallas_call x1, Pallas kernels, attend(): pl.pallas_call(attend_kernel, out_shape=(jax.ShapeDtypeStruct((rows, head...  61.1 us
    unnamed x4, local copies, waits for them, and re-layouts  22.7 us
    reduce_scatter x1, waiting for transfers between devices, on_device(): lax.psum_scatter(owned.reshape(blocks_dev * BLOCK, width), 'head', scatte...  21.8 us
    all_to_all x1, starting transfers between devices, on_device(): lax.all_to_all(request, 'seq', split_axis=0, concat_axis=0, tiled=True)  9.61 us
  transfers between devices with their start and end apart: 2, of which 1 were waited for; matrix products, arithmetic and copies ran while one was open for 9% of the time, Pallas kernels for 0%

profile of v3, /device:TPU:1, one launch (start us, length us, event | category | flops | bytes accessed | tf_op | source)
XLA Modules:
  0.0 281.7 jit_solution(5872751160556502669)
XLA Ops:
  8.0 0.8 copy.24
  8.8 0.1 eq.39
  8.9 0.5 fusion
  9.4 0.1 reduce_or.12
  9.5 0.3 reduce-window.9
  9.8 0.1 slice.22
  9.9 0.1 reshape.81
  10.0 0.1 slice_reduce_fusion
  10.1 0.1 add_bitcast_fusion
  10.2 0.6 slice.24
  10.7 0.1 broadcast.92
  10.8 0.1 reshape.82
  11.6 0.8 fusion.3
  12.3 0.7 copy.25
  13.0 9.6 %all-to-all-start = ((s32[32,1,2]{2,1,0:T(1,128)}), s32[32,1,2]{2,1,0:T(1,128)S(1)}, u32[]{:S(2)}, u32[]{:S(2)}) async-start(s32[32,1,2]{2,1,0:T(1,128)} %copy.25), calls=%async_computation.1 | async-start | bytes 32768 | tf_op jit(solution)/shard_map/all_to_all | solution.py:654
  22.7 1.2 select_reduce_fusion.slot_ref
  23.9 1.2 and_select_fusion.limit_ref
  25.1 0.2 select_reduce_fusion.1
  25.3 4.3 %copy.27 = bf16[2048,576]{1,0:T(8,128)(2,1)} copy(bf16[2048,576]{0,1:T(8,128)(2,1)} %param.10) | data formatting | bytes 4718592 | tf_op args[1]
  29.7 9.0 %copy.29.q_hbm = bf16[128,32,576]{2,1,0:T(8,128)(2,1)} copy(bf16[128,32,576]{0,2,1:T(8,128)(2,1)} %param.9) | data formatting | bytes 9437184 | tf_op args[0]
  38.7 0.1 copy.26
  38.7 0.5 broadcast_maximum_fusion.asked_ref
  39.2 1.2 slice_bitcast_fusion
  41.1 67.0 %fetch.1 = (bf16[4,4,17,16,576]{4,3,2,1,0:T(8,128)(2,1)}, bf16[4,32,16,576]{3,2,1,0:T(8,128)(2,1)S(1)}) custom-call(s32[32]{0:T(128)} %broadcast_maximum_fusion.asked_ref, s32[17]{0:T(128)S(1)} %bitcast.29, bf16[32,64,576]{2,1,0:T(8,128)(2,1)} %bitcast.23), custom_call_target="tpu_custom_call" | custom-call | tf_op jit(solution)/shard_map/fetch/pallas_call | solution.py:173
  108.2 61.1 %attend.1 = (bf16[128,32,512]{2,1,0:T(8,128)(2,1)}, bf16[128,32,576]{2,1,0:T(8,128)(2,1)}, bf16[4,4,17,16,576]{4,3,2,1,0:T(8,128)(2,1)}, bf16[4,15,64,576]{3,2,1,0:T(8,128)(2,1)}) custom-call(s32[1]{0:T(128)} %add.49.count_ref, s32[768]{0:T(1024)} %select_reduce_fusion.slot_ref, s32[128]{0:T(128)} %and_select_fusion.limit_ref, ...), custom_call_target="tpu_custom_call" | custom-call | tf_op jit(solution)/shard_map/attend/pallas_call | solution.py:576
  169.3 0.0 reduce-scatter.5.cloned.1.call-start
  169.4 67.7 %give_back.1.src = bf16[4,32,16,576]{3,2,1,0:T(8,128)(2,1)} custom-call(s32[32]{0:T(128)} %get-tuple-element.50.place_ref, bf16[4,4,17,16,576]{4,3,2,1,0:T(8,128)(2,1)} %get-tuple-element.28.dk_v, bf16[15,64,576]{2,1,0:T(8,128)(2,1)} %get-tuple-element.55.far_v), custom_call_target="tpu_custom_call" | custom-call | tf_op jit(solution)/shard_map/give_back/pallas_call | solution.py:305
  237.1 4.4 %add_blocks.1 = bf16[32,64,576]{2,1,0:T(8,128)(2,1)} custom-call(s32[32]{0:T(128)} %get-tuple-element.52.asked_ref, bf16[4,32,16,576]{3,2,1,0:T(8,128)(2,1)} %give_back.1.src), custom_call_target="tpu_custom_call" | custom-call | tf_op jit(solution)/shard_map/add_blocks/pallas_call | solution.py:342
  241.4 0.0 reduce-scatter.5.cloned.1.call-update
  241.5 8.6 %copy.30 = bf16[128,32,576]{0,2,1:T(8,128)(2,1)} copy(bf16[128,32,576]{2,1,0:T(8,128)(2,1)} %get-tuple-element.48) | data formatting | bytes 9437184
  250.1 21.8 %reduce-scatter.5.cloned.1.call-done.src = bf16[512,576]{1,0:T(8,128)(2,1)} async-done(((bf16[2048,576]{1,0:T(8,128)(2,1)}), bf16[512,576]{1,0:T(8,128)(2,1)}) %reduce-scatter.5.cloned.1.call-update) | async-done | bytes 589840 | tf_op jit(solution)/shard_map/reduce_scatter | solution.py:684
  271.9 2.4 widen_turned.1
  (10 shorter events, 0.1 us)
Async XLA Ops:
  13.0 25.6 %all-to-all-start = ((s32[32,1,2]{2,1,0:T(1,128)}), s32[32,1,2]{2,1,0:T(1,128)S(1)}, u32[]{:S(2)}, u32[]{:S(2)}) async-start(s32[32,1,2]{2,1,0:T(1,128)} %copy.25), calls=%async_computation.1 | async-start | bytes 32768 | tf_op jit(solution)/shard_map/all_to_all | solution.py:654
  169.3 102.6 %reduce-scatter.5.cloned.1.call-start = ((), (), s32[]{:S(2)}) async-start(), calls=%async_computation.5 | async-start | bytes 3276800 | tf_op jit(solution)/shard_map/reduce_scatter | solution.py:684
Sparse Core Ops, SparseCore 1:
  241.6 30.3 reduce-scatter.4

commit v4 on v3

--- a/solution.py
+++ b/solution.py
@@ -18,8 +18,8 @@
 BF16 = jnp.bfloat16
 F32 = jnp.float32
 COPY_ROWS = 16
-STEP_ROWS = 8
-CHUNK = 8
+STEP_ROWS = 16
+CHUNK = 16
 HBM = pl.BlockSpec(memory_space=pl.ANY)
 SMEM = pl.BlockSpec(memory_space=pltpu.SMEM)
 VMEM = pl.BlockSpec(memory_space=pltpu.VMEM)
@@ -192,9 +192,9 @@
     )(asked, owner_at, blocks)
 
 
-def give_back_kernel(place_ref, dk_v, far_v, out_hbm,
-                     sum_r, sum_l, one_l, one_r, two_l, two_r, places_v, back_v,
-                     x_send, x_recv, a_send, a_recv, own_sem):
+def give_back_kernel(place_ref, dk_hbm, far_v, out_hbm,
+                     dk_v, sum_r, sum_l, one_l, one_r, two_l, two_r, places_v, back_v,
+                     x_send, x_recv, a_send, a_recv, own_sem, load_sem):
     chunks, parts, near, rows, _ = dk_v.shape
     seq_count = back_v.shape[1]
     cut = (near + 1) // 2
@@ -221,8 +221,8 @@
 
     def first(c):
         return (
-            over_x(c, 0, dk_v.at[c, far, pl.ds(0, cut)], one_l.at[c], right),
-            over_x(c, 1, dk_v.at[c, far, pl.ds(cut, near - cut)], one_r.at[c], left),
+            over_x(c, 0, dk_hbm.at[c, far, pl.ds(0, cut)], one_l.at[c], right),
+            over_x(c, 1, dk_hbm.at[c, far, pl.ds(cut, near - cut)], one_r.at[c], left),
         )
 
     def second(c):
@@ -234,6 +234,9 @@
     def own(c):
         return pltpu.make_async_copy(back_v.at[c, me], out_hbm.at[c, me], own_sem.at[c])
 
+    def load(c):
+        return pltpu.make_async_copy(dk_hbm.at[c], dk_v.at[c], load_sem.at[c])
+
     def begin(c):
         for x in first(c):
             x.start()
@@ -241,6 +244,7 @@
     def add_far(c):
         from_left, from_right = first(c)
         to_right, to_left = second(c)
+        load(c).wait()
         from_left.wait_recv()
         sum_r[c, :cut] = (dk_v[c, right, :cut].astype(F32) + one_l[c].astype(F32)).astype(BF16)
         sum_r[c, cut:] = dk_v[c, right, cut:]
@@ -278,6 +282,8 @@
 
     begin(0)
     begin(1)
+    for c in range(chunks):
+        load(c).start()
     for c in range(chunks + 1):
         if c < chunks:
             add_far(c)
@@ -305,12 +311,13 @@
     return pl.pallas_call(
         give_back_kernel,
         out_shape=jax.ShapeDtypeStruct((chunks, seq_count, rows, width), BF16),
-        in_specs=[SMEM, VMEM, VMEM],
+        in_specs=[SMEM, HBM, VMEM],
         out_specs=HBM,
-        scratch_shapes=piece + [
+        scratch_shapes=[pltpu.VMEM(dk.shape, BF16)] + piece + [
             pltpu.VMEM((near + far.shape[0], rows, width), BF16),
             pltpu.VMEM((chunks, seq_count, rows, width), BF16),
             dma((chunks, 4)), dma((chunks, 4)), dma((chunks,)), dma((chunks,)), dma((chunks,)),
+            dma((chunks,)),
         ],
         compiler_params=pltpu.CompilerParams(
             vmem_limit_bytes=VMEM_BYTES, collective_id=2, has_side_effects=True

time: 282 us -> 288 us (1.021)
  Pallas kernels: 203 us -> 206 us
    pallas_call x1, Pallas kernels: 61.1 us -> 67.9 us  [attend(): pl.pallas_call(attend_kernel, out_shape=(jax.ShapeDtypeStruct((rows, head...]
    pallas_call x1, Pallas kernels: 67.7 us -> 64.7 us  [give_back(): pl.pallas_call(give_back_kernel, out_shape=jax.ShapeDtypeStruct((chunks,...]
where the time goes in v4:
time: 288 us; the launch traced here: 287 us
  Pallas kernels  206 us (72%)
  local copies, waits for them, and re-layouts  24.8 us (9%)
  waiting for transfers between devices  22.8 us (8%)
  between operations  16.8 us (6%)
  starting transfers between devices  9.83 us (3%)
  other arithmetic  6.08 us (2%)
    pallas_call x1, Pallas kernels, attend(): pl.pallas_call(attend_kernel, out_shape=(jax.ShapeDtypeStruct((rows, head...  67.9 us
    pallas_call x1, Pallas kernels, fetch(): pl.pallas_call(fetch_kernel, out_shape=(jax.ShapeDtypeStruct((CHUNKS, par...  67 us
    pallas_call x1, Pallas kernels, give_back(): pl.pallas_call(give_back_kernel, out_shape=jax.ShapeDtypeStruct((chunks,...  64.7 us
    unnamed x4, local copies, waits for them, and re-layouts  22.8 us
    reduce_scatter x1, waiting for transfers between devices, on_device(): lax.psum_scatter(owned.reshape(blocks_dev * BLOCK, width), 'head', scatte...  22.7 us
    all_to_all x1, starting transfers between devices, on_device(): lax.all_to_all(request, 'seq', split_axis=0, concat_axis=0, tiled=True)  9.61 us
  transfers between devices with their start and end apart: 2, of which 1 were waited for; matrix products, arithmetic and copies ran while one was open for 9% of the time, Pallas kernels for 0%

profile of v4, /device:TPU:1, one launch (start us, length us, event | category | flops | bytes accessed | tf_op | source)
XLA Modules:
  0.0 286.7 jit_solution(8576974158511219371)
XLA Ops:
  8.0 0.8 copy.24
  8.8 0.1 eq.39
  8.9 0.5 fusion
  9.4 0.1 reduce_or.12
  9.5 0.3 reduce-window.9
  9.8 0.1 slice.22
  9.9 0.1 reshape.81
  10.0 0.1 slice_reduce_fusion
  10.1 0.1 add_bitcast_fusion
  10.2 0.6 slice.24
  10.7 0.1 broadcast.92
  10.8 0.1 reshape.82
  11.6 0.8 fusion.3
  12.3 0.7 copy.25
  13.0 9.6 %all-to-all-start = ((s32[32,1,2]{2,1,0:T(1,128)}), s32[32,1,2]{2,1,0:T(1,128)S(1)}, u32[]{:S(2)}, u32[]{:S(2)}) async-start(s32[32,1,2]{2,1,0:T(1,128)} %copy.25), calls=%async_computation.1 | async-start | bytes 32768 | tf_op jit(solution)/shard_map/all_to_all | solution.py:661
  22.7 1.2 select_reduce_fusion.slot_ref
  23.9 1.2 and_select_fusion.limit_ref
  25.1 0.2 select_reduce_fusion.1
  25.3 4.3 %copy.27 = bf16[2048,576]{1,0:T(8,128)(2,1)} copy(bf16[2048,576]{0,1:T(8,128)(2,1)} %param.10) | data formatting | bytes 4718592 | tf_op args[1]
  29.7 9.0 %copy.29.q_hbm = bf16[128,32,576]{2,1,0:T(8,128)(2,1)} copy(bf16[128,32,576]{0,2,1:T(8,128)(2,1)} %param.9) | data formatting | bytes 9437184 | tf_op args[0]
  38.7 0.1 copy.26
  38.7 0.5 broadcast_maximum_fusion.asked_ref
  39.2 1.2 slice_bitcast_fusion
  41.1 67.0 %fetch.1 = (bf16[4,4,17,16,576]{4,3,2,1,0:T(8,128)(2,1)}, bf16[4,32,16,576]{3,2,1,0:T(8,128)(2,1)S(1)}) custom-call(s32[32]{0:T(128)} %broadcast_maximum_fusion.asked_ref, s32[17]{0:T(128)S(1)} %bitcast.29, bf16[32,64,576]{2,1,0:T(8,128)(2,1)} %bitcast.23), custom_call_target="tpu_custom_call" | custom-call | tf_op jit(solution)/shard_map/fetch/pallas_call | solution.py:173
  108.2 67.9 %attend.1 = (bf16[128,32,512]{2,1,0:T(8,128)(2,1)}, bf16[128,32,576]{2,1,0:T(8,128)(2,1)}, bf16[4,4,17,16,576]{4,3,2,1,0:T(8,128)(2,1)}, bf16[4,15,64,576]{3,2,1,0:T(8,128)(2,1)}) custom-call(s32[1]{0:T(128)} %add.49.count_ref, s32[768]{0:T(1024)} %select_reduce_fusion.slot_ref, s32[128]{0:T(128)} %and_select_fusion.limit_ref, ...), custom_call_target="tpu_custom_call" | custom-call | tf_op jit(solution)/shard_map/attend/pallas_call | solution.py:583
  176.1 0.2 reduce-scatter.5.cloned.1.call-start
  176.3 64.7 %give_back.1.src = bf16[4,32,16,576]{3,2,1,0:T(8,128)(2,1)} custom-call(s32[32]{0:T(128)} %get-tuple-element.50.place_ref, bf16[4,4,17,16,576]{4,3,2,1,0:T(8,128)(2,1)} %get-tuple-element.28.dk_hbm, bf16[15,64,576]{2,1,0:T(8,128)(2,1)} %get-tuple-element.55.far_v), custom_call_target="tpu_custom_call" | custom-call | tf_op jit(solution)/shard_map/give_back/pallas_call | solution.py:311
  241.0 4.4 %add_blocks.1 = bf16[32,64,576]{2,1,0:T(8,128)(2,1)} custom-call(s32[32]{0:T(128)} %get-tuple-element.52.asked_ref, bf16[4,32,16,576]{3,2,1,0:T(8,128)(2,1)} %give_back.1.src), custom_call_target="tpu_custom_call" | custom-call | tf_op jit(solution)/shard_map/add_blocks/pallas_call | solution.py:349
  245.4 0.0 reduce-scatter.5.cloned.1.call-update
  245.4 8.7 %copy.30 = bf16[128,32,576]{0,2,1:T(8,128)(2,1)} copy(bf16[128,32,576]{2,1,0:T(8,128)(2,1)} %get-tuple-element.48) | data formatting | bytes 9437184
  254.2 22.7 %reduce-scatter.5.cloned.1.call-done.src = bf16[512,576]{1,0:T(8,128)(2,1)} async-done(((bf16[2048,576]{1,0:T(8,128)(2,1)}), bf16[512,576]{1,0:T(8,128)(2,1)}) %reduce-scatter.5.cloned.1.call-update) | async-done | bytes 589840 | tf_op jit(solution)/shard_map/reduce_scatter | solution.py:691
  276.9 2.4 widen_turned.1
  (10 shorter events, 0.1 us)
Async XLA Ops:
  13.0 25.6 %all-to-all-start = ((s32[32,1,2]{2,1,0:T(1,128)}), s32[32,1,2]{2,1,0:T(1,128)S(1)}, u32[]{:S(2)}, u32[]{:S(2)}) async-start(s32[32,1,2]{2,1,0:T(1,128)} %copy.25), calls=%async_computation.1 | async-start | bytes 32768 | tf_op jit(solution)/shard_map/all_to_all | solution.py:661
  176.1 100.8 %reduce-scatter.5.cloned.1.call-start = ((), (), s32[]{:S(2)}) async-start(), calls=%async_computation.5 | async-start | bytes 3276800 | tf_op jit(solution)/shard_map/reduce_scatter | solution.py:691
Sparse Core Ops, SparseCore 1:
  245.5 31.3 reduce-scatter.4

commit v5 on v4

--- a/solution.py
+++ b/solution.py
@@ -19,7 +19,7 @@
 F32 = jnp.float32
 COPY_ROWS = 16
 STEP_ROWS = 16
-CHUNK = 16
+CHUNK = 8
 HBM = pl.BlockSpec(memory_space=pl.ANY)
 SMEM = pl.BlockSpec(memory_space=pltpu.SMEM)
 VMEM = pl.BlockSpec(memory_space=pltpu.VMEM)

time: 288 us -> 280 us (0.972)
  Pallas kernels: 206 us -> 200 us
    pallas_call x1, Pallas kernels: 67.9 us -> 62.1 us  [attend(): pl.pallas_call(attend_kernel, out_shape=(jax.ShapeDtypeStruct((rows, head...]
where the time goes in v5:
time: 280 us; the launch traced here: 279 us
  Pallas kernels  200 us (71%)
  local copies, waits for them, and re-layouts  24.7 us (9%)
  waiting for transfers between devices  22 us (8%)
  between operations  16.8 us (6%)
  starting transfers between devices  9.83 us (4%)
  other arithmetic  6.08 us (2%)
    pallas_call x1, Pallas kernels, fetch(): pl.pallas_call(fetch_kernel, out_shape=(jax.ShapeDtypeStruct((CHUNKS, par...  67 us
    pallas_call x1, Pallas kernels, give_back(): pl.pallas_call(give_back_kernel, out_shape=jax.ShapeDtypeStruct((chunks,...  63.8 us
    pallas_call x1, Pallas kernels, attend(): pl.pallas_call(attend_kernel, out_shape=(jax.ShapeDtypeStruct((rows, head...  62.1 us
    unnamed x4, local copies, waits for them, and re-layouts  22.7 us
    reduce_scatter x1, waiting for transfers between devices, on_device(): lax.psum_scatter(owned.reshape(blocks_dev * BLOCK, width), 'head', scatte...  22 us
    all_to_all x1, starting transfers between devices, on_device(): lax.all_to_all(request, 'seq', split_axis=0, concat_axis=0, tiled=True)  9.61 us
  transfers between devices with their start and end apart: 2, of which 1 were waited for; matrix products, arithmetic and copies ran while one was open for 9% of the time, Pallas kernels for 0%

profile of v5, /device:TPU:1, one launch (start us, length us, event | category | flops | bytes accessed | tf_op | source)
XLA Modules:
  0.0 279.2 jit_solution(2190300715214377172)
XLA Ops:
  8.0 0.8 copy.24
  8.8 0.1 eq.39
  8.9 0.5 fusion
  9.4 0.1 reduce_or.12
  9.5 0.3 reduce-window.9
  9.8 0.1 slice.22
  9.9 0.1 reshape.81
  10.0 0.1 slice_reduce_fusion
  10.1 0.1 add_bitcast_fusion
  10.2 0.6 slice.24
  10.7 0.1 broadcast.92
  10.8 0.1 reshape.82
  11.6 0.8 fusion.3
  12.3 0.7 copy.25
  13.0 9.6 %all-to-all-start = ((s32[32,1,2]{2,1,0:T(1,128)}), s32[32,1,2]{2,1,0:T(1,128)S(1)}, u32[]{:S(2)}, u32[]{:S(2)}) async-start(s32[32,1,2]{2,1,0:T(1,128)} %copy.25), calls=%async_computation.1 | async-start | bytes 32768 | tf_op jit(solution)/shard_map/all_to_all | solution.py:661
  22.7 1.2 select_reduce_fusion.slot_ref
  23.9 1.2 and_select_fusion.limit_ref
  25.1 0.2 select_reduce_fusion.1
  25.3 4.3 %copy.27 = bf16[2048,576]{1,0:T(8,128)(2,1)} copy(bf16[2048,576]{0,1:T(8,128)(2,1)} %param.10) | data formatting | bytes 4718592 | tf_op args[1]
  29.7 9.0 %copy.29.q_hbm = bf16[128,32,576]{2,1,0:T(8,128)(2,1)} copy(bf16[128,32,576]{0,2,1:T(8,128)(2,1)} %param.9) | data formatting | bytes 9437184 | tf_op args[0]
  38.7 0.1 copy.26
  38.7 0.5 broadcast_maximum_fusion.asked_ref
  39.2 1.2 slice_bitcast_fusion
  41.1 67.0 %fetch.1 = (bf16[4,4,17,16,576]{4,3,2,1,0:T(8,128)(2,1)}, bf16[4,32,16,576]{3,2,1,0:T(8,128)(2,1)S(1)}) custom-call(s32[32]{0:T(128)} %broadcast_maximum_fusion.asked_ref, s32[17]{0:T(128)S(1)} %bitcast.29, bf16[32,64,576]{2,1,0:T(8,128)(2,1)} %bitcast.23), custom_call_target="tpu_custom_call" | custom-call | tf_op jit(solution)/shard_map/fetch/pallas_call | solution.py:173
  108.2 62.1 %attend.1 = (bf16[128,32,512]{2,1,0:T(8,128)(2,1)}, bf16[128,32,576]{2,1,0:T(8,128)(2,1)}, bf16[4,4,17,16,576]{4,3,2,1,0:T(8,128)(2,1)}, bf16[4,15,64,576]{3,2,1,0:T(8,128)(2,1)}) custom-call(s32[1]{0:T(128)} %add.49.count_ref, s32[768]{0:T(1024)} %select_reduce_fusion.slot_ref, s32[128]{0:T(128)} %and_select_fusion.limit_ref, ...), custom_call_target="tpu_custom_call" | custom-call | tf_op jit(solution)/shard_map/attend/pallas_call | solution.py:583
  170.4 0.2 reduce-scatter.5.cloned.1.call-start
  170.6 63.8 %give_back.1.src = bf16[4,32,16,576]{3,2,1,0:T(8,128)(2,1)} custom-call(s32[32]{0:T(128)} %get-tuple-element.50.place_ref, bf16[4,4,17,16,576]{4,3,2,1,0:T(8,128)(2,1)} %get-tuple-element.28.dk_hbm, bf16[15,64,576]{2,1,0:T(8,128)(2,1)} %get-tuple-element.55.far_v), custom_call_target="tpu_custom_call" | custom-call | tf_op jit(solution)/shard_map/give_back/pallas_call | solution.py:311
  234.4 4.4 %add_blocks.1 = bf16[32,64,576]{2,1,0:T(8,128)(2,1)} custom-call(s32[32]{0:T(128)} %get-tuple-element.52.asked_ref, bf16[4,32,16,576]{3,2,1,0:T(8,128)(2,1)} %give_back.1.src), custom_call_target="tpu_custom_call" | custom-call | tf_op jit(solution)/shard_map/add_blocks/pallas_call | solution.py:349
  238.8 0.0 reduce-scatter.5.cloned.1.call-update
  238.8 8.7 %copy.30 = bf16[128,32,576]{0,2,1:T(8,128)(2,1)} copy(bf16[128,32,576]{2,1,0:T(8,128)(2,1)} %get-tuple-element.48) | data formatting | bytes 9437184
  247.5 22.0 %reduce-scatter.5.cloned.1.call-done.src = bf16[512,576]{1,0:T(8,128)(2,1)} async-done(((bf16[2048,576]{1,0:T(8,128)(2,1)}), bf16[512,576]{1,0:T(8,128)(2,1)}) %reduce-scatter.5.cloned.1.call-update) | async-done | bytes 589840 | tf_op jit(solution)/shard_map/reduce_scatter | solution.py:691
  269.4 2.4 widen_turned.1
  (10 shorter events, 0.1 us)
Async XLA Ops:
  13.0 25.6 %all-to-all-start = ((s32[32,1,2]{2,1,0:T(1,128)}), s32[32,1,2]{2,1,0:T(1,128)S(1)}, u32[]{:S(2)}, u32[]{:S(2)}) async-start(s32[32,1,2]{2,1,0:T(1,128)} %copy.25), calls=%async_computation.1 | async-start | bytes 32768 | tf_op jit(solution)/shard_map/all_to_all | solution.py:661
  170.4 99.0 %reduce-scatter.5.cloned.1.call-start = ((), (), s32[]{:S(2)}) async-start(), calls=%async_computation.5 | async-start | bytes 3276800 | tf_op jit(solution)/shard_map/reduce_scatter | solution.py:691
Sparse Core Ops, SparseCore 1:
  238.9 30.5 reduce-scatter.4
